TPU v7x, 128 devices: a whole 4x4x4 slice. The times are simulated.
128 devices in a mesh: latent: 16 (over y, z), dp: 8 (over x, core).
Axes of the slice: x: 4, y: 4, z: 4, core: 2. Of those that a mesh axis runs over, the one named last changes fastest.
Arguments:
- residual: bfloat16 [1024, 4608], P('dp', 'latent'), may hold values from -6 to 6
- encoder: bfloat16 [4608, 131072], P(None, ('latent', 'dp')), may hold values from -0.09375 to 0.09375
- encoder_bias: float32 [131072], P(('latent', 'dp')), may hold values from -3 to 3
- thresholds: int32 [131072], P(('latent', 'dp')), may hold values from 32 to 255
- decoder: bfloat16 [131072, 4608], P(('latent', 'dp')), may hold values from -0.03125 to 0.03125
- decoder_bias: float32 [4608], replicated, may hold values from -4 to 4
- probes: bfloat16 [131072, 64], P(('latent', 'dp')), may hold values from -0.03125 to 0.03125
- probe_bias: float32 [64], replicated, may hold values from -4 to 4
- labels: int32 [1024, 64], replicated, may hold values 0 or 1
Outputs:
- error: float32 [1024], P(('latent', 'dp'))
- probe_grad: float32 [131072, 64], P(('latent', 'dp'))
- bias_grad: float32 [64], replicated
- mean_loss: float32 [], replicated
All inputs are finite; a program needn't handle non-finite values.
Results may differ from a plain program's by a relative error of at most 0.00075.
Values may be sent and summed in bfloat16 or wider, within the bound.
No kernel may reach another device: no remote copies, remote signals or barrier semaphores. Data moves between devices by JAX's collectives and lax.ppermute only.
A program may use at most 192 MiB of HBM per device.

v0:
```python
import jax
import jax.numpy as jnp
from jax import lax
from jax.sharding import PartitionSpec as P

softness = 0.1
levels = 256.0


def on_device(
    residual, encoder, encoder_bias, thresholds, decoder, decoder_bias, probes, probe_bias, labels
):
    per_group = residual.shape[0]
    features = lax.all_gather(residual, "latent", axis=1, tiled=True)
    whole = lax.all_gather(features, "dp", axis=0, tiled=True)
    tokens = whole.shape[0]
    probe_count = probes.shape[1]
    preact = jnp.dot(whole, encoder, preferred_element_type=jnp.float32) + encoder_bias
    cutoff = thresholds.astype(jnp.float32) / levels
    active = (preact * jax.nn.sigmoid((preact - cutoff) / softness)).astype(jnp.bfloat16)
    devices = lax.axis_size(("latent", "dp"))
    row_count = tokens // devices
    position = lax.axis_index(("latent", "dp"))
    row_start = position * row_count
    logits = (
        lax.psum(jnp.dot(active, probes, preferred_element_type=jnp.float32), ("latent", "dp"))
        + probe_bias
    )
    target = labels.astype(jnp.float32)
    slopes = (jax.nn.sigmoid(logits) - target).astype(jnp.bfloat16)
    mean_loss = jnp.sum(jax.nn.softplus(logits) - target * logits) / (tokens * probe_count)
    received = lax.psum_scatter(
        jnp.dot(active, decoder, preferred_element_type=jnp.float32),
        ("latent", "dp"),
        scatter_dimension=0,
        tiled=True,
    )
    recon = received + decoder_bias
    own_rows = lax.dynamic_slice_in_dim(whole, row_start, row_count, 0).astype(jnp.float32)
    error = jnp.mean((own_rows - recon) ** 2, axis=1)
    probe_grad = (
        lax.dot_general(
            active, slopes, (((0,), (0,)), ((), ())), preferred_element_type=jnp.float32
        )
        / per_group
    )
    bias_grad = jnp.sum(slopes.astype(jnp.float32), axis=0) / per_group
    return (error, probe_grad, bias_grad, mean_loss)


def solution(mesh):
    in_specs = (
        P("dp", "latent"),
        P(None, ("latent", "dp")),
        P(("latent", "dp")),
        P(("latent", "dp")),
        P(("latent", "dp"), None),
        P(),
        P(("latent", "dp"), None),
        P(),
        P(),
    )
    out_specs = (P(("latent", "dp")), P(("latent", "dp"), None), P(), P())
    return jax.shard_map(
        on_device, mesh=mesh, in_specs=in_specs, out_specs=out_specs, check_vma=False
    )
```

profile of v0, /device:TPU:26, one launch (start us, length us, event | category | flops | bytes accessed | tf_op | source)
XLA Modules:
  0.0 517.4 jit_solution(391923084118251194)
XLA Ops:
  7.2 0.0 copy-start
  7.2 0.0 all-gather.3.cloned.1.call-start
  7.2 0.7 all-gather.3.cloned.1.call-update
  7.9 0.0 all-gather.5.cloned.1.call-start
  8.0 47.3 %all-gather.3.cloned.1.call-done = bf16[128,4608]{0,1:T(8,128)(2,1)} async-done(((bf16[128,288]{0,1:T(8,128)(2,1)}), bf16[128,4608]{0,1:T(8,128)(2,1)}) %all-gather.3.cloned.1.call-update) | async-done | bytes 1179664 | tf_op jit(solution)/shard_map/all_gather | solution.py:14
  55.2 2.4 copy.14
  57.7 0.0 all-gather.5.cloned.1.call-update
  57.7 0.0 all-reduce.2.cloned.1.call-start
  57.7 0.7 convert_multiply_fusion
  58.4 52.3 %all-gather.5.cloned.1.call-done = bf16[1024,4608]{1,0:T(8,128)(2,1)} async-done(((bf16[128,4608]{1,0:T(8,128)(2,1)}), bf16[1024,4608]{1,0:T(8,128)(2,1)}) %all-gather.5.cloned.1.call-update) | async-done | bytes 9437200 | tf_op jit(solution)/shard_map/all_gather | solution.py:15
  110.8 15.9 %multiply_convert_fusion = bf16[1024,1024]{1,0:T(8,128)(2,1)S(1)} fusion(f32[1024]{0:T(1024)S(1)} %convert_multiply_fusion, f32[1024]{0:T(1024)} %param.11, bf16[1024,4608]{1,0:T(8,128)(2,1)} %all-gather.5.cloned.1.call-done, bf16[4608,1024]{1,0:T(8,128)(2,1)} %param.10), kind=kOutput, calls=%fused_computation | convolution fusion | flops 9672065024 | bytes 20979712 | tf_op jit(solution)/shard_map/dot_general | solution.py:18
  126.6 0.0 copy-done
  126.7 1.5 fusion.3
  128.1 0.0 all-reduce.2.cloned.1.call-update
  128.1 0.0 reduce-scatter.2.cloned.1.call-start
  128.2 16.1 %fusion.2 = f32[1024,4608]{1,0:T(8,128)} fusion(bf16[1024,1024]{1,0:T(8,128)(2,1)S(1)} %multiply_convert_fusion, bf16[1024,4608]{1,0:T(8,128)(2,1)} %param.13), kind=kOutput, calls=%fused_computation.11 | convolution fusion | flops 9663676416 | bytes 30408704 | tf_op jit(solution)/shard_map/dot_general | solution.py:33
  144.3 0.0 copy-start.1
  144.3 0.0 copy-start.3
  144.3 0.0 copy-start.2
  144.3 0.0 reduce-scatter.2.cloned.1.call-update
  144.3 125.6 %all-reduce.2.cloned.1.call-done = f32[1024,64]{0,1:T(8,128)} async-done(((f32[1024,64]{0,1:T(8,128)}), f32[1024,64]{0,1:T(8,128)}) %all-reduce.2.cloned.1.call-update) | async-done | bytes 262160 | tf_op jit(solution)/shard_map/psum | solution.py:26
  269.9 0.0 copy-done.1
  269.9 0.0 copy-done.3
  269.9 1.9 convert_reduce_fusion
  272.4 0.5 broadcast_multiply_fusion
  273.0 1.2 convolution_multiply_fusion
  274.2 234.0 %reduce-scatter.2.cloned.1.call-done = f32[8,4608]{1,0:T(8,128)} async-done(((f32[1024,4608]{1,0:T(8,128)}), f32[8,4608]{1,0:T(8,128)}) %reduce-scatter.2.cloned.1.call-update) | async-done | bytes 147472 | tf_op jit(solution)/shard_map/reduce_scatter | solution.py:32
  508.1 0.0 copy-done.2
  508.1 1.1 multiply_reduce_fusion
  509.3 0.5 broadcast_multiply_fusion.1
Async XLA Ops:
  7.2 119.5 %copy-start = (bf16[1024,64]{0,1:T(8,128)(2,1)S(1)}, bf16[1024,64]{0,1:T(8,128)(2,1)}, u32[]{:S(2)}) copy-start(bf16[1024,64]{0,1:T(8,128)(2,1)} %param.15) | copy-start | bytes 393220
  7.2 48.0 %all-gather.3.cloned.1.call-start = ((), (), s32[]{:S(2)}) async-start(), calls=%async_computation.1 | async-start | bytes 1253376 | tf_op jit(solution)/shard_map/all_gather | solution.py:14
  7.9 102.8 %all-gather.5.cloned.1.call-start = ((), (), s32[]{:S(2)}) async-start(), calls=%async_computation.2 | async-start | bytes 10616832 | tf_op jit(solution)/shard_map/all_gather | solution.py:15
  57.7 212.2 %all-reduce.2.cloned.1.call-start = ((), (), s32[]{:S(2)}) async-start(), calls=%async_computation.4 | async-start | bytes 524288 | tf_op jit(solution)/shard_map/psum | solution.py:26
  128.1 380.0 %reduce-scatter.2.cloned.1.call-start = ((), (), s32[]{:S(2)}) async-start(), calls=%async_computation.3 | async-start | bytes 19021824 | tf_op jit(solution)/shard_map/reduce_scatter | solution.py:32
  144.3 125.6 %copy-start.1 = (s32[1024,64]{0,1:T(8,128)S(1)}, s32[1024,64]{0,1:T(8,128)}, u32[]{:S(2)}) copy-start(s32[1024,64]{0,1:T(8,128)} %param.17) | copy-start | bytes 786436
  144.3 125.6 %copy-start.3 = (f32[64]{0:T(128)S(1)}, f32[64]{0:T(128)}, u32[]{:S(2)}) copy-start(f32[64]{0:T(128)} %param.16) | copy-start | bytes 772
  144.3 363.9 %copy-start.2 = (f32[4608]{0:T(1024)S(1)}, f32[4608]{0:T(1024)}, u32[]{:S(2)}) copy-start(f32[4608]{0:T(1024)} %param.14) | copy-start | bytes 55300
Sparse Core Ops, SparseCore 0:
  10.2 44.9 all-gather.2
  57.8 52.9 all-gather.4
  128.3 141.6 all-reduce.1
  275.1 233.0 reduce-scatter.1
where the time goes:
time: 520 us; the launch traced here: 517 us
  waiting for transfers between devices  460 us (88%)
  matrix products  34.6 us (7%)
  between operations  15.6 us (3%)
    reduce_scatter x1, waiting for transfers between devices, on_device(): lax.psum_scatter(jnp.dot(active, decoder, preferred_element_type=jnp.floa...  234 us
    psum x1, waiting for transfers between devices, on_device(): lax.psum(jnp.dot(active, probes, preferred_element_type=jnp.float32), ('l...  126 us
    all_gather x1, waiting for transfers between devices, on_device(): whole = lax.all_gather(features, 'dp', axis=0, tiled=True)  52.3 us
    all_gather x1, waiting for transfers between devices, on_device(): features = lax.all_gather(residual, 'latent', axis=1, tiled=True)  47.3 us
    dot_general x1, matrix products, on_device(): jnp.dot(active, decoder, preferred_element_type=jnp.float32)  16.1 us
    dot_general x1, matrix products, on_device(): jnp.dot(whole, encoder, preferred_element_type=jnp.float32) + encoder_bias  15.9 us
  transfers between devices with their start and end apart: 4, of which 4 were waited for; matrix products, arithmetic and copies ran while one was open for 4% of the time, Pallas kernels for 0%

commit v1 on v0

v1 whole, which is shorter than its diff:
```python
import functools

import jax
import jax.numpy as jnp
from jax import lax
from jax.experimental import pallas as pl
from jax.experimental.pallas import tpu as pltpu
from jax.sharding import PartitionSpec as P

softness = 0.1
levels = 256.0
AXES = ("latent", "dp")
F32 = jnp.float32
BF16 = jnp.bfloat16
KB = 1152
D = 4608
W = D + 128
W2 = D + 512
W3 = D + 1024
VMEM_LIMIT = 8 * 1024 * 1024


def flat(y, z, x, c):
    return ((y * 4 + z) * 4 + x) * 2 + c


def coords():
    for y in range(4):
        for z in range(4):
            for x in range(4):
                for c in range(2):
                    yield {"y": y, "z": z, "x": x}, c


def place(p, c):
    return flat(p["y"], p["z"], p["x"], c)


def pull_perm(axis0, axis1, step):
    pairs = []
    for p, c in coords():
        axis = (axis0, axis1)[c]
        q = dict(p)
        q[axis] = (p[axis] + step) % 4
        pairs.append((place(q, c), place(p, c)))
    return pairs


def pull(value, axis0, axis1, step):
    return lax.ppermute(value, AXES, pull_perm(axis0, axis1, step))


def swap(value):
    pairs = [(place(p, c), place(p, 1 - c)) for p, c in coords()]
    return lax.ppermute(value, AXES, pairs)


def absolute(parts, start):
    twice = jnp.stack(list(parts) * 2)
    return lax.dynamic_slice_in_dim(twice, lax.rem(4 - start, 4), 4, 0)


def relative(stacked, start):
    return lax.dynamic_slice_in_dim(jnp.concatenate([stacked, stacked], 0), start, 4, 0)


STAGES = (0, 1, 3, 2)


def encode_kernel(stage, count, tile, where, *refs):
    own, oth = refs[:count], refs[count : 2 * count]
    refs = refs[2 * count :]
    enc, bias, cut = refs[:3]
    acc = None if stage == STAGES[0] else refs[3]
    xa, ya = refs[-2:]
    core, y = where[0], where[1]
    depth = 4 // count

    def rows(step):
        return pl.ds(pl.multiple_of(lax.rem(y + step, 4) * KB, KB), KB)

    def work(by_x, by_y):
        @pl.loop(0, enc.shape[1] // tile)
        def _(n):
            cols = pl.ds(pl.multiple_of(n * tile, tile), tile)

            def activate(preact):
                gate = jax.nn.sigmoid((preact - cut[:, cols]) / softness)
                return (preact * gate).astype(BF16)

            pre = bias[:, cols] + sum(
                jnp.dot(
                    by_x[j // depth][j % depth], enc[rows(j), cols], preferred_element_type=F32
                )
                for j in range(4)
            )
            xa[:, cols] = activate(pre)
            for i in range(count):
                part = jnp.dot(
                    by_y[i][...].reshape(128 * depth, KB),
                    enc[rows(stage), cols],
                    preferred_element_type=F32,
                )
                span = slice(128 * depth * i, 128 * depth * (i + 1))
                if acc is not None:
                    part = part + acc[span, cols]
                if stage == STAGES[-1]:
                    ya[span, cols] = activate(part + bias[:, cols])
                else:
                    ya[span, cols] = part

    @pl.when(core == 0)
    def _():
        work(own, oth)

    @pl.when(core == 1)
    def _():
        work(oth, own)


def encode(stage, where, own, oth, enc, bias, cut, acc):
    lat = enc.shape[1]
    vmem = pl.BlockSpec(memory_space=pltpu.VMEM)
    args = [*own, *oth, enc, bias, cut]
    aliases = {}
    if acc is not None:
        args.append(acc)
        if stage != STAGES[-1]:
            aliases = {len(args): 1}
    return pl.pallas_call(
        functools.partial(encode_kernel, stage, len(own), 256),
        in_specs=[pl.BlockSpec(memory_space=pltpu.SMEM)] + [vmem] * len(args),
        out_specs=[vmem, vmem],
        out_shape=[
            jax.ShapeDtypeStruct((128, lat), BF16),
            jax.ShapeDtypeStruct((512, lat), BF16 if stage == STAGES[-1] else F32),
        ],
        input_output_aliases=aliases,
        compiler_params=pltpu.CompilerParams(vmem_limit_bytes=VMEM_LIMIT),
        cost_estimate=pl.CostEstimate(
            flops=2 * 256 * D * lat, bytes_accessed=0, transcendentals=0
        ),
        name="encode",
    )(where, *args)


def split(total):
    lane = lax.broadcasted_iota(jnp.int32, total.shape, total.ndim - 1)
    high = total.astype(BF16).astype(F32)
    return jnp.where(lane < 64, high, total - high)


def joined(pair):
    return pair + pltpu.roll(pair, 64, pair.ndim - 1)


def decode_kernel(tile, where, xa, ya, dec, probes, keep, send, lhs):
    core, pick = where[0], where[2]
    lhs[pl.ds(pl.multiple_of(core * 128, 128), 128), :] = xa[...]
    lhs[pl.ds(pl.multiple_of((1 - core) * 128, 128), 128), :] = ya[pick]
    logits = split(jnp.dot(lhs[...], probes[...], preferred_element_type=F32)).astype(BF16)
    keep[:, D:] = logits[:128]
    send[:, D:] = logits[128:]

    @pl.loop(0, D // tile)
    def _(n):
        cols = pl.ds(pl.multiple_of(n * tile, tile), tile)
        out = jnp.dot(lhs[...], dec[:, cols], preferred_element_type=F32).astype(BF16)
        keep[:, cols] = out[:128]
        send[:, cols] = out[128:]


def decode(where, xa, ya, dec, probes):
    lat = dec.shape[0]
    vmem = pl.BlockSpec(memory_space=pltpu.VMEM)
    return pl.pallas_call(
        functools.partial(decode_kernel, 768),
        in_specs=[pl.BlockSpec(memory_space=pltpu.SMEM)] + [vmem] * 4,
        out_specs=[vmem, vmem],
        scratch_shapes=[pltpu.VMEM((256, lat), BF16)],
        out_shape=[jax.ShapeDtypeStruct((128, W), BF16)] * 2,
        compiler_params=pltpu.CompilerParams(vmem_limit_bytes=VMEM_LIMIT),
        cost_estimate=pl.CostEstimate(
            flops=2 * 256 * D * lat, bytes_accessed=0, transcendentals=0
        ),
        name="decode",
    )(where, xa, ya, dec, probes)


def small_call(kernel, name, outs, *args, scalars=1, scratch=()):
    vmem = pl.BlockSpec(memory_space=pltpu.VMEM)
    smem = pl.BlockSpec(memory_space=pltpu.SMEM)
    return pl.pallas_call(
        kernel,
        in_specs=[smem] * scalars + [vmem] * (len(args) - scalars),
        out_specs=[vmem] * len(outs),
        out_shape=[jax.ShapeDtypeStruct(shape, kind) for shape, kind in outs],
        scratch_shapes=list(scratch),
        compiler_params=pltpu.CompilerParams(vmem_limit_bytes=VMEM_LIMIT),
        name=name,
    )(*args)


def pair_kernel(a, b, out):
    out[:, :D] = (a[:, :D].astype(F32) + b[:, :D].astype(F32)).astype(BF16)
    total = joined(a[:, D:].astype(F32) + b[:, D:].astype(F32))
    out[:, D:] = split(total).astype(BF16)


def pair_sum(a, b):
    return small_call(pair_kernel, "pair_sum", [((128, W), BF16)], a, b, scalars=0)[0]


def first_kernel(where, a0, b0, g1, g2, g3, *outs):
    spot = where[3]
    logits = sum(r[:, D:].astype(F32) for r in (a0, b0, g1, g2, g3))
    logits = split(joined(logits)).astype(BF16)
    for d, out in enumerate(outs):
        rows = pl.ds(pl.multiple_of(lax.rem(spot + d, 4) * 32, 32), 32)
        out[:, :D] = sum(r[rows, :D].astype(F32) for r in (a0, b0, g1, g2, g3)).astype(BF16)
        for k in range(4):
            out[:, D + 128 * k : D + 128 * (k + 1)] = logits[32 * k : 32 * (k + 1)]


def second_kernel(where, m0, g1, g2, g3, *refs):
    outs, total, wide = refs[:4], refs[4], refs[5]
    spot = where[4]

    def four(cols):
        a0, a1, a2, a3 = (r[:, cols].astype(F32) for r in (m0, g1, g2, g3))
        return (a0 + a2) + (a1 + a3)

    total[...] = four(slice(0, D))
    for k in range(4):
        cols = slice(D + 128 * k, D + 128 * (k + 1))
        l0, l1, l2, l3 = (joined(r[:, cols].astype(F32)) for r in (m0, g1, g2, g3))
        wide[32 * k : 32 * (k + 1), :] = (l0 + l2) + (l1 + l3)
    lane = lax.broadcasted_iota(jnp.int32, (8, 128), 1)
    packed = [
        jnp.where(lane < 64, wide[8 * i : 8 * i + 8, :], wide[64 + 8 * i : 72 + 8 * i, :])
        for i in range(8)
    ]
    for d, out in enumerate(outs):
        rows = pl.ds(pl.multiple_of(lax.rem(spot + d, 4) * 8, 8), 8)
        out[:, :D] = total[rows, :]
        for i in range(8):
            out[:, D + 128 * i : D + 128 * (i + 1)] = packed[i]


def third_kernel(m0, g1, g2, g3, tokens, bias, err, logits):
    def four(cols):
        a0, a1, a2, a3 = (r[:, cols] for r in (m0, g1, g2, g3))
        return (a0 + a2) + (a1 + a3)

    gap = tokens[...] - (four(slice(0, D)) + bias[...])
    err[...] = jnp.broadcast_to(jnp.sum(gap * gap, axis=1, keepdims=True) / D, err.shape)
    logits[...] = four(slice(D, W3))


def on_device(
    residual, encoder, encoder_bias, thresholds, decoder, decoder_bias, probes, probe_bias, labels
):
    per_group = residual.shape[0]
    lat = encoder.shape[1]
    pos = lax.axis_index(AXES)
    core = pos % 2
    x, z, y = (pos // 2) % 4, (pos // 8) % 4, pos // 32
    is0 = core == 0
    first = jnp.where(is0, x, y)
    second = jnp.where(is0, y, z)
    third = jnp.where(is0, z, x)

    parts = [residual] + [pull(residual, "z", "z", d) for d in (1, 2, 3)]
    unit = absolute(parts, z).transpose(1, 0, 2).reshape(per_group, KB)
    block = jnp.stack([unit] + [pull(unit, "y", "x", d) for d in (1, 2, 3)])
    own, oth = {0: [block]}, {0: [swap(block)]}
    near = {d: pull(block, "x", "y", d) for d in (1, 3)}

    cut = (thresholds.astype(F32) / levels)[None]
    bias = encoder_bias[None]
    where = jnp.stack([core, y]).astype(jnp.int32)
    xa = {}

    def run(stage, acc):
        xa[stage], acc = encode(stage, where, own[stage], oth[stage], encoder, bias, cut, acc)
        return acc

    acc = run(0, None)
    near, acc = lax.optimization_barrier((near, acc))
    far = [pull(near[1][:2], "x", "y", 1), pull(near[3][2:], "x", "y", 3)]
    for d in (1, 3):
        own[d], oth[d] = [near[d]], [swap(near[d])]
    acc = run(1, acc)
    acc = run(3, acc)
    far, acc = lax.optimization_barrier((far, acc))
    own[2], oth[2] = far, [swap(half) for half in far]
    acc = run(2, acc)
    ya = acc.reshape(4, 128, lat)

    probes2 = jnp.concatenate([probes, probes], axis=1)
    order = (2, 1, 3, 0)
    keep, got, message = {}, {}, {}
    for i, d in enumerate(order):
        spot = jnp.stack([core, y, lax.rem(y + d - x + 4, 4)]).astype(jnp.int32)
        left = xa[d]
        if i >= 2:
            left, message[order[i - 2]] = lax.optimization_barrier((left, message[order[i - 2]]))
        keep[d], send = decode(spot, left, ya, decoder, probes2)
        got[d] = swap(send)
        if d:
            message[d] = pair_sum(keep[d], got[d])
    mine = {d: pull(message[d], "x", "y", 4 - d) for d in (2, 1, 3)}

    where = jnp.stack([core, y, core, second, third]).astype(jnp.int32)
    m2 = small_call(
        first_kernel, "first_sum", [((32, W2), BF16)] * 4,
        where, keep[0], got[0], mine[1], mine[2], mine[3],
    )
    g2 = [pull(m2[d], "y", "z", 4 - d) for d in (1, 2, 3)]
    m3 = small_call(
        second_kernel, "second_sum", [((8, W3), F32)] * 4, where, m2[0], *g2,
        scratch=[pltpu.VMEM((32, D), F32), pltpu.VMEM((128, 128), F32)],
    )
    g3 = [pull(m3[d], "z", "x", 4 - d) for d in (1, 2, 3)]

    start = second * 32 + third * 8
    by_x = lax.dynamic_slice(block, (0, start, 0), (4, 8, KB))
    turn = lax.rem(y - x + 4, 4)

    def at(part, index):
        return lax.dynamic_slice(part, (index, start, 0), (1, 8, KB))

    low, high = at(far[0], jnp.minimum(turn, 1)), at(far[1], jnp.maximum(turn - 2, 0))
    by_y = jnp.concatenate(
        [at(block, turn), at(near[1], turn), jnp.where(turn < 2, low, high), at(near[3], turn)]
    )
    chosen = jnp.where(is0, by_x, by_y).astype(F32)
    tokens = relative(chosen, lax.rem(4 - y, 4)).transpose(1, 0, 2).reshape(8, D)

    err, packed = small_call(
        third_kernel, "third_sum", [((8, 128), F32), ((8, 1024), F32)],
        m3[0], *g3, tokens, decoder_bias[None], scalars=0,
    )
    owners = []
    for p, c in coords():
        s = (p["x"], p["y"], p["z"]) if c == 0 else (p["y"], p["z"], p["x"])
        owners.append((place(p, c), s[0] * 32 + c * 16 + s[1] * 4 + s[2]))
    error = lax.ppermute(err, AXES, owners)[:, 0]

    mine = absolute([packed] + [pull(packed, "x", "y", d) for d in (1, 2, 3)], first)
    theirs = swap(mine)
    both = jnp.stack([jnp.where(is0, mine, theirs), jnp.where(is0, theirs, mine)], 1)
    both = both.reshape(4, 2, 8, 8, 2, 64).transpose(0, 1, 4, 3, 2, 5).reshape(4, 2, 128, 64)
    logits = both + probe_bias
    target = labels.astype(F32).reshape(4, 2, 128, 64)
    slopes = (jax.nn.sigmoid(logits) - target).astype(BF16)
    mean_loss = jnp.sum(jax.nn.softplus(logits) - target * logits) / target.size
    bias_grad = jnp.sum(slopes.astype(F32), axis=(0, 1, 2)) / per_group
    turned = relative(slopes, x)
    active = jnp.concatenate([xa[0], xa[1], xa[2], xa[3], ya.reshape(512, lat)])
    turned = turned.transpose(1, 0, 2, 3).reshape(1024, 64)
    probe_grad = (
        lax.dot_general(active, turned, (((0,), (0,)), ((), ())), preferred_element_type=F32)
        / per_group
    )
    return (error, probe_grad, bias_grad, mean_loss)


def solution(mesh):
    in_specs = (
        P("dp", "latent"),
        P(None, ("latent", "dp")),
        P(("latent", "dp")),
        P(("latent", "dp")),
        P(("latent", "dp"), None),
        P(),
        P(("latent", "dp"), None),
        P(),
        P(),
    )
    out_specs = (P(("latent", "dp")), P(("latent", "dp"), None), P(), P())
    return jax.shard_map(
        on_device, mesh=mesh, in_specs=in_specs, out_specs=out_specs, check_vma=False
    )
```

time: 520 us -> 175 us (0.34)
  waiting for transfers between devices: 460 us -> 51 us
  Pallas kernels: 0 us -> 46.7 us
  starting transfers between devices: 0.16 us -> 36.7 us
  matrix products: 34.6 us -> 1.19 us
  local copies, waits for them, and re-layouts: 2.45 us -> 28.2 us
  between operations: 15.6 us -> 3.04 us
    reduce_scatter x1 -> x0, waiting for transfers between devices: 234 us -> none  [on_device(): lax.psum_scatter(jnp.dot(active, decoder, preferred_element_type=jnp.floa...]
    psum x1 -> x0, waiting for transfers between devices: 126 us -> none  [on_device(): lax.psum(jnp.dot(active, probes, preferred_element_type=jnp.float32), ('l...]
    all_gather x2 -> x0, waiting for transfers between devices: 99.6 us -> none  [the longest x1 52.3 us: on_device(): whole = lax.all_gather(features, 'dp', axis=0, tiled=True)]
    ppermute x0 -> x33, waiting for transfers between devices: none -> 51 us  [the longest x22 40.7 us: pull(): return lax.ppermute(value, AXES, pull_perm(axis0, axis1, step))]
    pallas_call x0 -> x14, Pallas kernels: none -> 46.7 us  [the longest x4 20.4 us: encode(): pl.pallas_call(functools.partial(encode_kernel, stage, len(own), 256), in...]
    ppermute x0 -> x33, starting transfers between devices: none -> 36.7 us  [the longest x22 30.5 us: pull(): return lax.ppermute(value, AXES, pull_perm(axis0, axis1, step))]
    dot_general x4 -> x1, matrix products: 34.6 us -> 1.19 us  [on_device(): lax.dot_general(active, turned, (((0,), (0,)), ((), ())), preferred_eleme...]
    unnamed x8 -> x83, local copies, waits for them, and re-layouts: 0.02 us -> 22.6 us
  transfers between devices with their start and end apart: 4 -> 33, of which waited for: 4 -> 19; matrix products, arithmetic and copies ran while one was open for 4% -> 7% of each run, Pallas kernels for 0% -> 18%
where the time goes in v1:
time: 175 us; the launch traced here: 174 us
  waiting for transfers between devices  51 us (29%)
  Pallas kernels  46.7 us (27%)
  starting transfers between devices  36.7 us (21%)
  local copies, waits for them, and re-layouts  28.2 us (16%)
  other arithmetic  7.17 us (4%)
  between operations  3.04 us (2%)
    ppermute x22, waiting for transfers between devices, pull(): return lax.ppermute(value, AXES, pull_perm(axis0, axis1, step))  40.7 us
    ppermute x22, starting transfers between devices, pull(): return lax.ppermute(value, AXES, pull_perm(axis0, axis1, step))  30.5 us
    unnamed x83, local copies, waits for them, and re-layouts  22.6 us
    pallas_call x4, Pallas kernels, encode(): pl.pallas_call(functools.partial(encode_kernel, stage, len(own), 256), in...  20.4 us
    pallas_call x4, Pallas kernels, decode(): pl.pallas_call(functools.partial(decode_kernel, 768), in_specs=[pl.BlockS...  18.6 us
    pallas_call x6, Pallas kernels, small_call(): pl.pallas_call(kernel, in_specs=[smem] * scalars + [vmem] * (len(args) -...  7.81 us
    ppermute x1, waiting for transfers between devices, on_device(): error = lax.ppermute(err, AXES, owners)[:, 0]  7.39 us
    ppermute x1, starting transfers between devices, on_device(): error = lax.ppermute(err, AXES, owners)[:, 0]  3.76 us
  transfers between devices with their start and end apart: 33, of which 19 were waited for; matrix products, arithmetic and copies ran while one was open for 7% of the time, Pallas kernels for 18%

profile of v1, /device:TPU:26, one launch (start us, length us, event | category | flops | bytes accessed | tf_op | source)
XLA Modules:
  0.0 174.1 jit_solution(12700706372249265935)
XLA Ops:
  0.6 4.1 %collective-permute-start = (bf16[128,288]{0,1:T(8,128)(2,1)}, bf16[128,288]{0,1:T(8,128)(2,1)S(1)}, u32[]{:S(2)}, u32[]{:S(2)}) collective-permute-start(bf16[128,288]{0,1:T(8,128)(2,1)} %param.9), channel_id=1, source_target_pairs={{8,0},{9,1},{10,2},{11,3},{12,4},{13,5},{14,6},{15,7},{16,8},{17,9... | collective-permute-start | bytes 221192 | tf_op jit(solution)/shard_map/ppermute | solution.py:50
  4.7 1.9 %collective-permute-start.1 = (bf16[128,288]{0,1:T(8,128)(2,1)}, bf16[128,288]{0,1:T(8,128)(2,1)S(1)}, u32[]{:S(2)}, u32[]{:S(2)}) collective-permute-start(bf16[128,288]{0,1:T(8,128)(2,1)} %param.9), channel_id=1, source_target_pairs={{16,0},{17,1},{18,2},{19,3},{20,4},{21,5},{22,6},{23,7},{24,8},{25... | collective-permute-start | bytes 221192 | tf_op jit(solution)/shard_map/ppermute | solution.py:50
  7.5 3.3 %collective-permute-done.1 = bf16[128,288]{0,1:T(8,128)(2,1)S(1)} collective-permute-done((bf16[128,288]{0,1:T(8,128)(2,1)}, bf16[128,288]{0,1:T(8,128)(2,1)S(1)}, u32[]{:S(2)}, u32[]{:S(2)}) %collective-permute-start.1) | collective-permute-done | bytes 73760 | tf_op jit(solution)/shard_map/ppermute | solution.py:50
  13.0 2.6 %collective-permute-start.4 = (bf16[128,1152]{1,0:T(8,128)(2,1)S(1)}, bf16[128,1152]{1,0:T(8,128)(2,1)S(1)}, u32[]{:S(2)}, u32[]{:S(2)}) collective-permute-start(bf16[128,1152]{1,0:T(8,128)(2,1)S(1)} %copy.21), channel_id=1, source_target_pairs={{64,0},{5,1},{66,2},{7,3},{68,4},{1,5},{70,6},{3,7},{72,8},{13,9},... | collective-permute-start | bytes 884744 | tf_op jit(solution)/shard_map/ppermute | solution.py:50
  15.8 3.7 %collective-permute-done.5 = bf16[128,1152]{1,0:T(8,128)(2,1)S(1)} collective-permute-done((bf16[128,1152]{1,0:T(8,128)(2,1)S(1)}, bf16[128,1152]{1,0:T(8,128)(2,1)S(1)}, u32[]{:S(2)}, u32[]{:S(2)}) %collective-permute-start.5) | collective-permute-done | bytes 294944 | tf_op jit(solution)/shard_map/ppermute | solution.py:50
  21.3 3.1 %collective-permute-done.3 = bf16[128,1152]{1,0:T(8,128)(2,1)S(1)} collective-permute-done((bf16[128,1152]{1,0:T(8,128)(2,1)S(1)}, bf16[128,1152]{1,0:T(8,128)(2,1)S(1)}, u32[]{:S(2)}, u32[]{:S(2)}) %collective-permute-start.3) | collective-permute-done | bytes 294944 | tf_op jit(solution)/shard_map/ppermute | solution.py:50
  29.7 3.7 %copy-done = bf16[4608,1024]{1,0:T(8,128)(2,1)S(1)} copy-done((bf16[4608,1024]{1,0:T(8,128)(2,1)S(1)}, bf16[4608,1024]{1,0:T(8,128)(2,1)}, u32[]{:S(2)}) %copy-start) | copy-done | bytes 9437208
  34.7 5.0 %encode.4 = (bf16[128,1024]{1,0:T(8,128)(2,1)S(1)}, f32[512,1024]{1,0:T(8,128)S(1)}) custom-call(s32[2]{0:T(128)S(1)} %pad_add_fusion.2.where, bf16[4,128,1152]{2,1,0:T(8,128)(2,1)} %pad_maximum_fusion.refs_0_, bf16[4,128,1152]{2,1,0:T(8,128)(2,1)S(1)} %copy-done.7, bf16[4608,1024]{1,0:T(8,128)(2,1)S(1)} %copy-done, f32[1,1024]{1,0:T(1,128)S(1)} %bitcast.101, ...), custom_call_target="tpu_custom_call" | custom-call | flops 2415919104 | tf_op jit(solution)/shard_map/encode/pallas_call | solution.py:130
  39.7 2.4 %collective-permute-done.8.refs_0_ = bf16[4,128,1152]{2,1,0:T(8,128)(2,1)} collective-permute-done((bf16[4,128,1152]{2,1,0:T(8,128)(2,1)}, bf16[4,128,1152]{2,1,0:T(8,128)(2,1)}, u32[]{:S(2)}, u32[]{:S(2)}) %collective-permute-start.8) | collective-permute-done | bytes 1179680 | tf_op jit(solution)/shard_map/ppermute | solution.py:50
  48.5 4.9 %encode.5 = (bf16[128,1024]{1,0:T(8,128)(2,1)S(1)}, f32[512,1024]{1,0:T(8,128)S(1)}) custom-call(s32[2]{0:T(128)S(1)} %pad_add_fusion.2.where, bf16[4,128,1152]{2,1,0:T(8,128)(2,1)} %collective-permute-done.7.refs_0_, bf16[4,128,1152]{2,1,0:T(8,128)(2,1)S(1)} %collective-permute-done.9.refs_1_, ...), custom_call_target="tpu_custom_call", output_to_operand_aliasing={{1}: (6, {})} | custom-call | flops 2415919104 | tf_op jit(solution)/shard_map/encode/pallas_call | solution.py:130
  53.4 5.0 %encode.6 = (bf16[128,1024]{1,0:T(8,128)(2,1)S(1)}, f32[512,1024]{1,0:T(8,128)S(1)}) custom-call(s32[2]{0:T(128)S(1)} %pad_add_fusion.2.where, bf16[4,128,1152]{2,1,0:T(8,128)(2,1)} %collective-permute-done.8.refs_0_, bf16[4,128,1152]{2,1,0:T(8,128)(2,1)S(1)} %collective-permute-done.12.refs_1_, ...), custom_call_target="tpu_custom_call", output_to_operand_aliasing={{1}: (6, {})} | custom-call | flops 2415919104 | tf_op jit(solution)/shard_map/encode/pallas_call | solution.py:130
  61.6 3.7 %copy-done.2 = bf16[4608,1024]{1,0:T(8,128)(2,1)S(1)} copy-done((bf16[4608,1024]{1,0:T(8,128)(2,1)S(1)}, bf16[4608,1024]{1,0:T(8,128)(2,1)}, u32[]{:S(2)}) %copy-start.2) | copy-done | bytes 9437208
  66.3 5.5 %encode.7 = (bf16[128,1024]{1,0:T(8,128)(2,1)S(1)}, bf16[512,1024]{1,0:T(8,128)(2,1)S(1)}) custom-call(s32[2]{0:T(128)S(1)} %pad_add_fusion.2.where, bf16[2,128,1152]{2,1,0:T(8,128)(2,1)} %collective-permute-done.10.refs_0_, bf16[2,128,1152]{2,1,0:T(8,128)(2,1)S(1)} %copy-done.18, bf16[2,128,1152]{2,1,0:T(8,128)(2,1)} %collective-permute-done.13.refs_2_, ...), custom_call_target="tpu_custom_call" | custom-call | flops 2415919104 | tf_op jit(solution)/shard_map/encode/pallas_call | solution.py:130
  71.8 3.8 %copy-done.3 = bf16[1024,4608]{1,0:T(8,128)(2,1)S(1)} copy-done((bf16[1024,4608]{1,0:T(8,128)(2,1)S(1)}, bf16[1024,4608]{1,0:T(8,128)(2,1)}, u32[]{:S(2)}) %copy-start.3) | copy-done | bytes 9437208
  75.6 4.4 %decode.6 = (bf16[128,4736]{1,0:T(8,128)(2,1)S(1)}, bf16[128,4736]{1,0:T(8,128)(2,1)S(1)}) custom-call(s32[3]{0:T(128)S(1)} %get-tuple-element.80.where, bf16[128,1024]{1,0:T(8,128)(2,1)S(1)} %get-tuple-element.59.xa, bf16[4,128,1024]{2,1,0:T(8,128)(2,1)S(1)} %bitcast.92, bf16[1024,4608]{1,0:T(8,128)(2,1)S(1)} %copy-done.3, ...), custom_call_target="tpu_custom_call" | custom-call | flops 2415919104 | tf_op jit(solution)/shard_map/decode/pallas_call | solution.py:176
  80.2 4.4 %decode.4 = (bf16[128,4736]{1,0:T(8,128)(2,1)S(1)}, bf16[128,4736]{1,0:T(8,128)(2,1)S(1)}) custom-call(s32[3]{0:T(128)S(1)} %get-tuple-element.81.where, bf16[128,1024]{1,0:T(8,128)(2,1)S(1)} %copy-done.11, bf16[4,128,1024]{2,1,0:T(8,128)(2,1)S(1)} %bitcast.93, bf16[1024,4608]{1,0:T(8,128)(2,1)S(1)} %copy-done.3, bf16[1024,128]{1,0:T(8,128)(2,1)S(1)} %pad_maximum_fusion.1.probes), custom_call_target="tpu_custom_call" | custom-call | flops 2415919104 | tf_op jit(solution)/shard_map/decode/pallas_call | solution.py:176
  85.7 4.4 %decode.7 = (bf16[128,4736]{1,0:T(8,128)(2,1)S(1)}, bf16[128,4736]{1,0:T(8,128)(2,1)S(1)}) custom-call(s32[3]{0:T(128)S(1)} %get-tuple-element.76.where, bf16[128,1024]{1,0:T(8,128)(2,1)S(1)} %get-tuple-element.63.xa, bf16[4,128,1024]{2,1,0:T(8,128)(2,1)S(1)} %bitcast.94, bf16[1024,4608]{1,0:T(8,128)(2,1)S(1)} %bitcast.91, ...), custom_call_target="tpu_custom_call" | custom-call | flops 2415919104 | tf_op jit(solution)/shard_map/decode/pallas_call | solution.py:176
  90.3 2.3 %collective-permute-start.19 = (bf16[128,4736]{1,0:T(8,128)(2,1)S(1)}, bf16[128,4736]{1,0:T(8,128)(2,1)}, u32[]{:S(2)}, u32[]{:S(2)}) collective-permute-start(bf16[128,4736]{1,0:T(8,128)(2,1)S(1)} %pair_sum.4), channel_id=1, source_target_pairs={{4,0},{65,1},{6,2},{67,3},{0,4},{69,5},{2,6},{71,7},{12,8},{73,9},... | collective-permute-start | bytes 3637256 | tf_op jit(solution)/shard_map/ppermute | solution.py:50
  94.2 5.4 %decode.5 = (bf16[128,4736]{1,0:T(8,128)(2,1)S(1)}, bf16[128,4736]{1,0:T(8,128)(2,1)}) custom-call(s32[3]{0:T(128)S(1)} %get-tuple-element.82.where, bf16[128,1024]{1,0:T(8,128)(2,1)S(1)} %copy-done.14, bf16[4,128,1024]{2,1,0:T(8,128)(2,1)S(1)} %bitcast.95, bf16[1024,4608]{1,0:T(8,128)(2,1)S(1)} %bitcast.91, bf16[1024,128]{1,0:T(8,128)(2,1)S(1)} %pad_maximum_fusion.1.probes), custom_call_target="tpu_custom_call" | custom-call | flops 2415919104 | tf_op jit(solution)/shard_map/decode/pallas_call | solution.py:176
  104.6 1.9 %copy.29 = s32[1024,64]{1,0:T(8,128)} copy(s32[1024,64]{0,1:T(8,128)} %param.17) | data formatting | bytes 524288 | tf_op args[8]
  106.6 1.9 %convert_element_type.18 = f32[1024,64]{1,0:T(8,128)} convert(s32[1024,64]{1,0:T(8,128)} %copy.29) | non-fusion elementwise | flops 65536 | bytes 524288 | tf_op jit(solution)/shard_map/convert_element_type | solution.py:355
  112.7 8.6 %collective-permute-done.17.g1 = bf16[128,4736]{1,0:T(8,128)(2,1)} collective-permute-done((bf16[128,4736]{1,0:T(8,128)(2,1)S(1)}, bf16[128,4736]{1,0:T(8,128)(2,1)}, u32[]{:S(2)}, u32[]{:S(2)}) %collective-permute-start.17) | collective-permute-done | bytes 1212448 | tf_op jit(solution)/shard_map/ppermute | solution.py:50
  122.8 3.8 %first_sum.1 = (bf16[32,5120]{1,0:T(8,128)(2,1)S(1)}, bf16[32,5120]{1,0:T(8,128)(2,1)S(1)}, bf16[32,5120]{1,0:T(8,128)(2,1)S(1)}, bf16[32,5120]{1,0:T(8,128)(2,1)S(1)}) custom-call(s32[5]{0:T(128)S(1)} %stack.116.where, bf16[128,4736]{1,0:T(8,128)(2,1)S(1)} %copy-done.5, bf16[128,4736]{1,0:T(8,128)(2,1)} %collective-permute-done.16.b0, ...), custom_call_target="tpu_custom_call" | custom-call | tf_op jit(solution)/shard_map/first_sum/pallas_call | solution.py:193
  130.1 3.6 %collective-permute-done.22.g1 = bf16[32,5120]{1,0:T(8,128)(2,1)S(1)} collective-permute-done((bf16[32,5120]{1,0:T(8,128)(2,1)S(1)}, bf16[32,5120]{1,0:T(8,128)(2,1)S(1)}, u32[]{:S(2)}, u32[]{:S(2)}) %collective-permute-start.22) | collective-permute-done | bytes 327712 | tf_op jit(solution)/shard_map/ppermute | solution.py:50
  133.7 3.0 %collective-permute-done.23.g2 = bf16[32,5120]{1,0:T(8,128)(2,1)S(1)} collective-permute-done((bf16[32,5120]{1,0:T(8,128)(2,1)S(1)}, bf16[32,5120]{1,0:T(8,128)(2,1)S(1)}, u32[]{:S(2)}, u32[]{:S(2)}) %collective-permute-start.23) | collective-permute-done | bytes 327712 | tf_op jit(solution)/shard_map/ppermute | solution.py:50
  136.7 3.4 %collective-permute-done.24.g3 = bf16[32,5120]{1,0:T(8,128)(2,1)S(1)} collective-permute-done((bf16[32,5120]{1,0:T(8,128)(2,1)S(1)}, bf16[32,5120]{1,0:T(8,128)(2,1)S(1)}, u32[]{:S(2)}, u32[]{:S(2)}) %collective-permute-start.24) | collective-permute-done | bytes 327712 | tf_op jit(solution)/shard_map/ppermute | solution.py:50
  141.1 4.0 %collective-permute-start.26 = (f32[8,5632]{1,0:T(8,128)S(1)}, f32[8,5632]{1,0:T(8,128)S(1)}, u32[]{:S(2)}, u32[]{:S(2)}) collective-permute-start(f32[8,5632]{1,0:T(8,128)S(1)} %get-tuple-element.72), channel_id=1, source_target_pairs={{16,0},{5,1},{18,2},{7,3},{20,4},{1,5},{22,6},{3,7},{24,8},{13,9},... | collective-permute-start | bytes 540680 | tf_op jit(solution)/shard_map/ppermute | solution.py:50
  145.2 2.6 %collective-permute-done.25.g1 = f32[8,5632]{1,0:T(8,128)S(1)} collective-permute-done((f32[8,5632]{1,0:T(8,128)S(1)}, f32[8,5632]{1,0:T(8,128)S(1)}, u32[]{:S(2)}, u32[]{:S(2)}) %collective-permute-start.25) | collective-permute-done | bytes 180256 | tf_op jit(solution)/shard_map/ppermute | solution.py:50
  147.8 2.7 %collective-permute-done.26.g2 = f32[8,5632]{1,0:T(8,128)S(1)} collective-permute-done((f32[8,5632]{1,0:T(8,128)S(1)}, f32[8,5632]{1,0:T(8,128)S(1)}, u32[]{:S(2)}, u32[]{:S(2)}) %collective-permute-start.26) | collective-permute-done | bytes 180256 | tf_op jit(solution)/shard_map/ppermute | solution.py:50
  152.0 2.1 %collective-permute-start.30 = (f32[8,1024]{1,0:T(8,128)S(1)}, f32[8,1024]{1,0:T(8,128)S(1)}, u32[]{:S(2)}, u32[]{:S(2)}) collective-permute-start(f32[8,1024]{1,0:T(8,128)S(1)} %get-tuple-element.75), channel_id=1, source_target_pairs={{4,0},{65,1},{6,2},{67,3},{0,4},{69,5},{2,6},{71,7},{12,8},{73,9},... | collective-permute-start | bytes 98312 | tf_op jit(solution)/shard_map/ppermute | solution.py:50
  155.7 3.8 %collective-permute-start.28 = (f32[8,128]{1,0:T(8,128)S(1)}, f32[8,128]{1,0:T(8,128)S(1)}, u32[]{:S(2)}, u32[]{:S(2)}) collective-permute-start(f32[8,128]{1,0:T(8,128)S(1)} %get-tuple-element.74), channel_id=1, source_target_pairs={{0,0},{1,16},{2,32},{3,17},{4,64},{5,18},{6,96},{7,19},{8,1},{9,20... | collective-permute-start | bytes 12296 | tf_op jit(solution)/shard_map/ppermute | solution.py:348
  159.8 7.4 %collective-permute-done.28 = f32[8,128]{1,0:T(8,128)S(1)} collective-permute-done((f32[8,128]{1,0:T(8,128)S(1)}, f32[8,128]{1,0:T(8,128)S(1)}, u32[]{:S(2)}, u32[]{:S(2)}) %collective-permute-start.28) | collective-permute-done | bytes 4128 | tf_op jit(solution)/shard_map/ppermute | solution.py:348
  (168 shorter events, 48.9 us)
Async XLA Ops:
  0.6 6.9 %collective-permute-start = (bf16[128,288]{0,1:T(8,128)(2,1)}, bf16[128,288]{0,1:T(8,128)(2,1)S(1)}, u32[]{:S(2)}, u32[]{:S(2)}) collective-permute-start(bf16[128,288]{0,1:T(8,128)(2,1)} %param.9), channel_id=1, source_target_pairs={{8,0},{9,1},{10,2},{11,3},{12,4},{13,5},{14,6},{15,7},{16,8},{17,9... | collective-permute-start | bytes 221192 | tf_op jit(solution)/shard_map/ppermute | solution.py:50
  4.7 6.8 %collective-permute-start.2 = (bf16[128,288]{0,1:T(8,128)(2,1)}, bf16[128,288]{0,1:T(8,128)(2,1)S(1)}, u32[]{:S(2)}, u32[]{:S(2)}) collective-permute-start(bf16[128,288]{0,1:T(8,128)(2,1)} %param.9), channel_id=1, source_target_pairs={{24,0},{25,1},{26,2},{27,3},{28,4},{29,5},{30,6},{31,7},{0,8},{1,9... | collective-permute-start | bytes 221192 | tf_op jit(solution)/shard_map/ppermute | solution.py:50
  4.7 6.1 %collective-permute-start.1 = (bf16[128,288]{0,1:T(8,128)(2,1)}, bf16[128,288]{0,1:T(8,128)(2,1)S(1)}, u32[]{:S(2)}, u32[]{:S(2)}) collective-permute-start(bf16[128,288]{0,1:T(8,128)(2,1)} %param.9), channel_id=1, source_target_pairs={{16,0},{17,1},{18,2},{19,3},{20,4},{21,5},{22,6},{23,7},{24,8},{25... | collective-permute-start | bytes 221192 | tf_op jit(solution)/shard_map/ppermute | solution.py:50
  12.7 6.8 %collective-permute-start.5 = (bf16[128,1152]{1,0:T(8,128)(2,1)S(1)}, bf16[128,1152]{1,0:T(8,128)(2,1)S(1)}, u32[]{:S(2)}, u32[]{:S(2)}) collective-permute-start(bf16[128,1152]{1,0:T(8,128)(2,1)S(1)} %copy.21), channel_id=1, source_target_pairs={{96,0},{7,1},{98,2},{1,3},{100,4},{3,5},{102,6},{5,7},{104,8},{15,... | collective-permute-start | bytes 884744 | tf_op jit(solution)/shard_map/ppermute | solution.py:50
  13.0 8.3 %collective-permute-start.4 = (bf16[128,1152]{1,0:T(8,128)(2,1)S(1)}, bf16[128,1152]{1,0:T(8,128)(2,1)S(1)}, u32[]{:S(2)}, u32[]{:S(2)}) collective-permute-start(bf16[128,1152]{1,0:T(8,128)(2,1)S(1)} %copy.21), channel_id=1, source_target_pairs={{64,0},{5,1},{66,2},{7,3},{68,4},{1,5},{70,6},{3,7},{72,8},{13,9},... | collective-permute-start | bytes 884744 | tf_op jit(solution)/shard_map/ppermute | solution.py:50
  15.6 8.8 %collective-permute-start.3 = (bf16[128,1152]{1,0:T(8,128)(2,1)S(1)}, bf16[128,1152]{1,0:T(8,128)(2,1)S(1)}, u32[]{:S(2)}, u32[]{:S(2)}) collective-permute-start(bf16[128,1152]{1,0:T(8,128)(2,1)S(1)} %copy.21), channel_id=1, source_target_pairs={{32,0},{3,1},{34,2},{5,3},{36,4},{7,5},{38,6},{1,7},{40,8},{11,9},... | collective-permute-start | bytes 884744 | tf_op jit(solution)/shard_map/ppermute | solution.py:50
  25.6 3.1 %collective-permute-start.6 = (bf16[4,128,1152]{2,1,0:T(8,128)(2,1)}, bf16[4,128,1152]{2,1,0:T(8,128)(2,1)S(1)}, u32[]{:S(2)}, u32[]{:S(2)}) collective-permute-start(bf16[4,128,1152]{2,1,0:T(8,128)(2,1)} %pad_maximum_fusion.refs_0_), channel_id=1, source_target_pairs={{0,1},{1,0},{2,3},{3,2},{4,5},{5,4},{6,7},{7,6},{8,9},{9,8},{10,11... | collective-permute-start | bytes 3538952 | tf_op jit(solution)/shard_map/ppermute | solution.py:55
  25.6 16.5 %collective-permute-start.8 = (bf16[4,128,1152]{2,1,0:T(8,128)(2,1)}, bf16[4,128,1152]{2,1,0:T(8,128)(2,1)}, u32[]{:S(2)}, u32[]{:S(2)}) collective-permute-start(bf16[4,128,1152]{2,1,0:T(8,128)(2,1)} %pad_maximum_fusion.refs_0_), channel_id=1, source_target_pairs={{6,0},{97,1},{0,2},{99,3},{2,4},{101,5},{4,6},{103,7},{14,8},{105,... | collective-permute-start | bytes 3538952 | tf_op jit(solution)/shard_map/ppermute | solution.py:50
  27.1 16.5 %collective-permute-start.7 = (bf16[4,128,1152]{2,1,0:T(8,128)(2,1)}, bf16[4,128,1152]{2,1,0:T(8,128)(2,1)}, u32[]{:S(2)}, u32[]{:S(2)}) collective-permute-start(bf16[4,128,1152]{2,1,0:T(8,128)(2,1)} %pad_maximum_fusion.refs_0_), channel_id=1, source_target_pairs={{2,0},{33,1},{4,2},{35,3},{6,4},{37,5},{0,6},{39,7},{10,8},{41,9},... | collective-permute-start | bytes 3538952 | tf_op jit(solution)/shard_map/ppermute | solution.py:50
  43.6 4.8 %collective-permute-start.9 = (bf16[4,128,1152]{2,1,0:T(8,128)(2,1)}, bf16[4,128,1152]{2,1,0:T(8,128)(2,1)S(1)}, u32[]{:S(2)}, u32[]{:S(2)}) collective-permute-start(bf16[4,128,1152]{2,1,0:T(8,128)(2,1)} %collective-permute-done.7.refs_0_), channel_id=1, source_target_pairs={{0,1},{1,0},{2,3},{3,2},{4,5},{5,4},{6,7},{7,6},{8,9},{9,8},{10,11... | collective-permute-start | bytes 3538952 | tf_op jit(solution)/shard_map/ppermute | solution.py:55
  43.6 9.7 %collective-permute-start.12 = (bf16[4,128,1152]{2,1,0:T(8,128)(2,1)}, bf16[4,128,1152]{2,1,0:T(8,128)(2,1)S(1)}, u32[]{:S(2)}, u32[]{:S(2)}) collective-permute-start(bf16[4,128,1152]{2,1,0:T(8,128)(2,1)} %collective-permute-done.8.refs_0_), channel_id=1, source_target_pairs={{0,1},{1,0},{2,3},{3,2},{4,5},{5,4},{6,7},{7,6},{8,9},{9,8},{10,11... | collective-permute-start | bytes 3538952 | tf_op jit(solution)/shard_map/ppermute | solution.py:55
  46.4 12.1 %collective-permute-start.11 = (bf16[2,128,1152]{2,1,0:T(8,128)(2,1)S(1)}, bf16[2,128,1152]{2,1,0:T(8,128)(2,1)S(1)}, u32[]{:S(2)}, u32[]{:S(2)}) collective-permute-start(bf16[2,128,1152]{2,1,0:T(8,128)(2,1)S(1)} %slice.10), channel_id=1, source_target_pairs={{6,0},{97,1},{0,2},{99,3},{2,4},{101,5},{4,6},{103,7},{14,8},{105,... | collective-permute-start | bytes 1769480 | tf_op jit(solution)/shard_map/ppermute | solution.py:50
  47.6 10.8 %collective-permute-start.10 = (bf16[2,128,1152]{2,1,0:T(8,128)(2,1)S(1)}, bf16[2,128,1152]{2,1,0:T(8,128)(2,1)}, u32[]{:S(2)}, u32[]{:S(2)}) collective-permute-start(bf16[2,128,1152]{2,1,0:T(8,128)(2,1)S(1)} %slice.9), channel_id=1, source_target_pairs={{2,0},{33,1},{4,2},{35,3},{6,4},{37,5},{0,6},{39,7},{10,8},{41,9},... | collective-permute-start | bytes 1769480 | tf_op jit(solution)/shard_map/ppermute | solution.py:50
  58.6 3.0 %collective-permute-start.14 = (bf16[2,128,1152]{2,1,0:T(8,128)(2,1)S(1)}, bf16[2,128,1152]{2,1,0:T(8,128)(2,1)}, u32[]{:S(2)}, u32[]{:S(2)}) collective-permute-start(bf16[2,128,1152]{2,1,0:T(8,128)(2,1)S(1)} %collective-permute-done.11.refs_1_), channel_id=1, source_target_pairs={{0,1},{1,0},{2,3},{3,2},{4,5},{5,4},{6,7},{7,6},{8,9},{9,8},{10,11... | collective-permute-start | bytes 1769480 | tf_op jit(solution)/shard_map/ppermute | solution.py:55
  80.0 5.0 %collective-permute-start.18 = (bf16[128,4736]{1,0:T(8,128)(2,1)S(1)}, bf16[128,4736]{1,0:T(8,128)(2,1)S(1)}, u32[]{:S(2)}, u32[]{:S(2)}) collective-permute-start(bf16[128,4736]{1,0:T(8,128)(2,1)S(1)} %get-tuple-element.61), channel_id=1, source_target_pairs={{0,1},{1,0},{2,3},{3,2},{4,5},{5,4},{6,7},{7,6},{8,9},{9,8},{10,11... | collective-permute-start | bytes 3637256 | tf_op jit(solution)/shard_map/ppermute | solution.py:55
  84.6 8.1 %collective-permute-start.15 = (bf16[128,4736]{1,0:T(8,128)(2,1)S(1)}, bf16[128,4736]{1,0:T(8,128)(2,1)S(1)}, u32[]{:S(2)}, u32[]{:S(2)}) collective-permute-start(bf16[128,4736]{1,0:T(8,128)(2,1)S(1)} %get-tuple-element.53), channel_id=1, source_target_pairs={{0,1},{1,0},{2,3},{3,2},{4,5},{5,4},{6,7},{7,6},{8,9},{9,8},{10,11... | collective-permute-start | bytes 3637256 | tf_op jit(solution)/shard_map/ppermute | solution.py:55
  90.1 11.0 %collective-permute-start.20 = (bf16[128,4736]{1,0:T(8,128)(2,1)S(1)}, bf16[128,4736]{1,0:T(8,128)(2,1)S(1)}, u32[]{:S(2)}, u32[]{:S(2)}) collective-permute-start(bf16[128,4736]{1,0:T(8,128)(2,1)S(1)} %get-tuple-element.65), channel_id=1, source_target_pairs={{0,1},{1,0},{2,3},{3,2},{4,5},{5,4},{6,7},{7,6},{8,9},{9,8},{10,11... | collective-permute-start | bytes 3637256 | tf_op jit(solution)/shard_map/ppermute | solution.py:55
  90.3 22.3 %collective-permute-start.19 = (bf16[128,4736]{1,0:T(8,128)(2,1)S(1)}, bf16[128,4736]{1,0:T(8,128)(2,1)}, u32[]{:S(2)}, u32[]{:S(2)}) collective-permute-start(bf16[128,4736]{1,0:T(8,128)(2,1)S(1)} %pair_sum.4), channel_id=1, source_target_pairs={{4,0},{65,1},{6,2},{67,3},{0,4},{69,5},{2,6},{71,7},{12,8},{73,9},... | collective-permute-start | bytes 3637256 | tf_op jit(solution)/shard_map/ppermute | solution.py:50
  93.3 28.0 %collective-permute-start.17 = (bf16[128,4736]{1,0:T(8,128)(2,1)S(1)}, bf16[128,4736]{1,0:T(8,128)(2,1)}, u32[]{:S(2)}, u32[]{:S(2)}) collective-permute-start(bf16[128,4736]{1,0:T(8,128)(2,1)S(1)} %pair_sum.3), channel_id=1, source_target_pairs={{6,0},{97,1},{0,2},{99,3},{2,4},{101,5},{4,6},{103,7},{14,8},{105,... | collective-permute-start | bytes 3637256 | tf_op jit(solution)/shard_map/ppermute | solution.py:50
  100.7 20.5 %collective-permute-start.16 = (bf16[128,4736]{1,0:T(8,128)(2,1)}, bf16[128,4736]{1,0:T(8,128)(2,1)}, u32[]{:S(2)}, u32[]{:S(2)}) collective-permute-start(bf16[128,4736]{1,0:T(8,128)(2,1)} %get-tuple-element.56), channel_id=1, source_target_pairs={{0,1},{1,0},{2,3},{3,2},{4,5},{5,4},{6,7},{7,6},{8,9},{9,8},{10,11... | collective-permute-start | bytes 3637256 | tf_op jit(solution)/shard_map/ppermute | solution.py:55
  102.9 18.6 %collective-permute-start.21 = (bf16[128,4736]{1,0:T(8,128)(2,1)}, bf16[128,4736]{1,0:T(8,128)(2,1)}, u32[]{:S(2)}, u32[]{:S(2)}) collective-permute-start(bf16[128,4736]{1,0:T(8,128)(2,1)} %pair_sum.5), channel_id=1, source_target_pairs={{2,0},{33,1},{4,2},{35,3},{6,4},{37,5},{0,6},{39,7},{10,8},{41,9},... | collective-permute-start | bytes 3637256 | tf_op jit(solution)/shard_map/ppermute | solution.py:50
  126.5 7.1 %collective-permute-start.22 = (bf16[32,5120]{1,0:T(8,128)(2,1)S(1)}, bf16[32,5120]{1,0:T(8,128)(2,1)S(1)}, u32[]{:S(2)}, u32[]{:S(2)}) collective-permute-start(bf16[32,5120]{1,0:T(8,128)(2,1)S(1)} %get-tuple-element.67), channel_id=1, source_target_pairs={{96,0},{25,1},{98,2},{27,3},{100,4},{29,5},{102,6},{31,7},{104,8},... | collective-permute-start | bytes 983048 | tf_op jit(solution)/shard_map/ppermute | solution.py:50
  128.0 8.7 %collective-permute-start.23 = (bf16[32,5120]{1,0:T(8,128)(2,1)S(1)}, bf16[32,5120]{1,0:T(8,128)(2,1)S(1)}, u32[]{:S(2)}, u32[]{:S(2)}) collective-permute-start(bf16[32,5120]{1,0:T(8,128)(2,1)S(1)} %get-tuple-element.68), channel_id=1, source_target_pairs={{64,0},{17,1},{66,2},{19,3},{68,4},{21,5},{70,6},{23,7},{72,8},{25... | collective-permute-start | bytes 983048 | tf_op jit(solution)/shard_map/ppermute | solution.py:50
  129.8 10.3 %collective-permute-start.24 = (bf16[32,5120]{1,0:T(8,128)(2,1)S(1)}, bf16[32,5120]{1,0:T(8,128)(2,1)S(1)}, u32[]{:S(2)}, u32[]{:S(2)}) collective-permute-start(bf16[32,5120]{1,0:T(8,128)(2,1)S(1)} %get-tuple-element.69), channel_id=1, source_target_pairs={{32,0},{9,1},{34,2},{11,3},{36,4},{13,5},{38,6},{15,7},{40,8},{17,... | collective-permute-start | bytes 983048 | tf_op jit(solution)/shard_map/ppermute | solution.py:50
  141.0 6.8 %collective-permute-start.25 = (f32[8,5632]{1,0:T(8,128)S(1)}, f32[8,5632]{1,0:T(8,128)S(1)}, u32[]{:S(2)}, u32[]{:S(2)}) collective-permute-start(f32[8,5632]{1,0:T(8,128)S(1)} %get-tuple-element.71), channel_id=1, source_target_pairs={{24,0},{7,1},{26,2},{1,3},{28,4},{3,5},{30,6},{5,7},{0,8},{15,9},{... | collective-permute-start | bytes 540680 | tf_op jit(solution)/shard_map/ppermute | solution.py:50
  141.1 9.4 %collective-permute-start.26 = (f32[8,5632]{1,0:T(8,128)S(1)}, f32[8,5632]{1,0:T(8,128)S(1)}, u32[]{:S(2)}, u32[]{:S(2)}) collective-permute-start(f32[8,5632]{1,0:T(8,128)S(1)} %get-tuple-element.72), channel_id=1, source_target_pairs={{16,0},{5,1},{18,2},{7,3},{20,4},{1,5},{22,6},{3,7},{24,8},{13,9},... | collective-permute-start | bytes 540680 | tf_op jit(solution)/shard_map/ppermute | solution.py:50
  145.1 5.5 %collective-permute-start.27 = (f32[8,5632]{1,0:T(8,128)S(1)}, f32[8,5632]{1,0:T(8,128)S(1)}, u32[]{:S(2)}, u32[]{:S(2)}) collective-permute-start(f32[8,5632]{1,0:T(8,128)S(1)} %get-tuple-element.73), channel_id=1, source_target_pairs={{8,0},{3,1},{10,2},{5,3},{12,4},{7,5},{14,6},{1,7},{16,8},{11,9},{... | collective-permute-start | bytes 540680 | tf_op jit(solution)/shard_map/ppermute | solution.py:50
  150.8 8.8 %collective-permute-start.31 = (f32[8,1024]{1,0:T(8,128)S(1)}, f32[8,1024]{1,0:T(8,128)S(1)}, u32[]{:S(2)}, u32[]{:S(2)}) collective-permute-start(f32[8,1024]{1,0:T(8,128)S(1)} %get-tuple-element.75), channel_id=1, source_target_pairs={{6,0},{97,1},{0,2},{99,3},{2,4},{101,5},{4,6},{103,7},{14,8},{105,... | collective-permute-start | bytes 98312 | tf_op jit(solution)/shard_map/ppermute | solution.py:50
  152.0 7.6 %collective-permute-start.30 = (f32[8,1024]{1,0:T(8,128)S(1)}, f32[8,1024]{1,0:T(8,128)S(1)}, u32[]{:S(2)}, u32[]{:S(2)}) collective-permute-start(f32[8,1024]{1,0:T(8,128)S(1)} %get-tuple-element.75), channel_id=1, source_target_pairs={{4,0},{65,1},{6,2},{67,3},{0,4},{69,5},{2,6},{71,7},{12,8},{73,9},... | collective-permute-start | bytes 98312 | tf_op jit(solution)/shard_map/ppermute | solution.py:50
  154.1 5.4 %collective-permute-start.29 = (f32[8,1024]{1,0:T(8,128)S(1)}, f32[8,1024]{1,0:T(8,128)S(1)}, u32[]{:S(2)}, u32[]{:S(2)}) collective-permute-start(f32[8,1024]{1,0:T(8,128)S(1)} %get-tuple-element.75), channel_id=1, source_target_pairs={{2,0},{33,1},{4,2},{35,3},{6,4},{37,5},{0,6},{39,7},{10,8},{41,9},... | collective-permute-start | bytes 98312 | tf_op jit(solution)/shard_map/ppermute | solution.py:50
  155.7 11.5 %collective-permute-start.28 = (f32[8,128]{1,0:T(8,128)S(1)}, f32[8,128]{1,0:T(8,128)S(1)}, u32[]{:S(2)}, u32[]{:S(2)}) collective-permute-start(f32[8,128]{1,0:T(8,128)S(1)} %get-tuple-element.74), channel_id=1, source_target_pairs={{0,0},{1,16},{2,32},{3,17},{4,64},{5,18},{6,96},{7,19},{8,1},{9,20... | collective-permute-start | bytes 12296 | tf_op jit(solution)/shard_map/ppermute | solution.py:348
  159.6 8.2 %collective-permute-start.32 = (f32[4,8,1024]{2,1,0:T(8,128)S(1)}, f32[4,8,1024]{2,1,0:T(8,128)S(1)}, u32[]{:S(2)}, u32[]{:S(2)}) collective-permute-start(f32[4,8,1024]{2,1,0:T(8,128)S(1)} %constant_dynamic-slice_fusion), channel_id=1, source_target_pairs={{0,1},{1,0},{2,3},{3,2},{4,5},{5,4},{6,7},{7,6},{8,9},{9,8},{10,11... | collective-permute-start | bytes 393224 | tf_op jit(solution)/shard_map/ppermute | solution.py:55
  (32 other events, 220.5 us)

commit v2 on v1

--- a/solution.py
+++ b/solution.py
@@ -18,6 +18,7 @@
 W2 = D + 512
 W3 = D + 1024
 VMEM_LIMIT = 8 * 1024 * 1024
+LITTLE = pl.CostEstimate(flops=1000000, bytes_accessed=0, transcendentals=0)
 
 
 def flat(y, z, x, c):
@@ -60,20 +61,47 @@
     return lax.dynamic_slice_in_dim(twice, lax.rem(4 - start, 4), 4, 0)
 
 
-def relative(stacked, start):
-    return lax.dynamic_slice_in_dim(jnp.concatenate([stacked, stacked], 0), start, 4, 0)
+def load_kernel(source, target, sems):
+    pieces = sems.shape[0]
+    rows = source.shape[0] // pieces
+    copies = []
+    for i in range(pieces):
+        span = slice(rows * i, rows * (i + 1))
+        copies.append(pltpu.make_async_copy(source.at[span], target.at[span], sems.at[i]))
+    for copy in copies:
+        copy.start()
+    for copy in copies:
+        copy.wait()
+
+
+def load(value):
+    held = pl.pallas_call(
+        load_kernel,
+        in_specs=[pl.BlockSpec(memory_space=pltpu.HBM)],
+        out_specs=pl.BlockSpec(memory_space=pltpu.VMEM),
+        out_shape=jax.ShapeDtypeStruct(value.shape, value.dtype),
+        scratch_shapes=[pltpu.SemaphoreType.DMA((4,))],
+        compiler_params=pltpu.CompilerParams(vmem_limit_bytes=VMEM_LIMIT),
+        cost_estimate=LITTLE,
+        name="load",
+    )(pltpu.with_memory_space_constraint(value, pltpu.HBM))
+    return near(held)
+
+
+def near(value):
+    return pltpu.with_memory_space_constraint(value, pltpu.VMEM)
 
 
 STAGES = (0, 1, 3, 2)
 
 
 def encode_kernel(stage, count, tile, where, *refs):
+    core, y = where[0], where[2]
     own, oth = refs[:count], refs[count : 2 * count]
     refs = refs[2 * count :]
     enc, bias, cut = refs[:3]
     acc = None if stage == STAGES[0] else refs[3]
     xa, ya = refs[-2:]
-    core, y = where[0], where[1]
     depth = 4 // count
 
     def rows(step):
@@ -85,7 +113,8 @@
             cols = pl.ds(pl.multiple_of(n * tile, tile), tile)
 
             def activate(preact):
-                gate = jax.nn.sigmoid((preact - cut[:, cols]) / softness)
+                cutoff = cut[:, cols].astype(F32) / levels
+                gate = jax.nn.sigmoid((preact - cutoff) / softness)
                 return (preact * gate).astype(BF16)
 
             pre = bias[:, cols] + sum(
@@ -137,9 +166,7 @@
         ],
         input_output_aliases=aliases,
         compiler_params=pltpu.CompilerParams(vmem_limit_bytes=VMEM_LIMIT),
-        cost_estimate=pl.CostEstimate(
-            flops=2 * 256 * D * lat, bytes_accessed=0, transcendentals=0
-        ),
+        cost_estimate=LITTLE,
         name="encode",
     )(where, *args)
 
@@ -154,8 +181,9 @@
     return pair + pltpu.roll(pair, 64, pair.ndim - 1)
 
 
-def decode_kernel(tile, where, xa, ya, dec, probes, keep, send, lhs):
-    core, pick = where[0], where[2]
+def decode_kernel(step, tile, where, xa, ya, dec, probes, keep, send, lhs):
+    core = where[0]
+    pick = lax.rem(where[2] + step - where[1] + 4, 4)
     lhs[pl.ds(pl.multiple_of(core * 128, 128), 128), :] = xa[...]
     lhs[pl.ds(pl.multiple_of((1 - core) * 128, 128), 128), :] = ya[pick]
     logits = split(jnp.dot(lhs[...], probes[...], preferred_element_type=F32)).astype(BF16)
@@ -170,19 +198,17 @@
         send[:, cols] = out[128:]
 
 
-def decode(where, xa, ya, dec, probes):
+def decode(step, where, xa, ya, dec, probes):
     lat = dec.shape[0]
     vmem = pl.BlockSpec(memory_space=pltpu.VMEM)
     return pl.pallas_call(
-        functools.partial(decode_kernel, 768),
+        functools.partial(decode_kernel, step, 768),
         in_specs=[pl.BlockSpec(memory_space=pltpu.SMEM)] + [vmem] * 4,
         out_specs=[vmem, vmem],
         scratch_shapes=[pltpu.VMEM((256, lat), BF16)],
         out_shape=[jax.ShapeDtypeStruct((128, W), BF16)] * 2,
         compiler_params=pltpu.CompilerParams(vmem_limit_bytes=VMEM_LIMIT),
-        cost_estimate=pl.CostEstimate(
-            flops=2 * 256 * D * lat, bytes_accessed=0, transcendentals=0
-        ),
+        cost_estimate=LITTLE,
         name="decode",
     )(where, xa, ya, dec, probes)
 
@@ -197,34 +223,51 @@
         out_shape=[jax.ShapeDtypeStruct(shape, kind) for shape, kind in outs],
         scratch_shapes=list(scratch),
         compiler_params=pltpu.CompilerParams(vmem_limit_bytes=VMEM_LIMIT),
+        cost_estimate=LITTLE,
         name=name,
     )(*args)
 
 
-def pair_kernel(a, b, out):
-    out[:, :D] = (a[:, :D].astype(F32) + b[:, :D].astype(F32)).astype(BF16)
-    total = joined(a[:, D:].astype(F32) + b[:, D:].astype(F32))
-    out[:, D:] = split(total).astype(BF16)
-
-
-def pair_sum(a, b):
-    return small_call(pair_kernel, "pair_sum", [((128, W), BF16)], a, b, scalars=0)[0]
-
-
-def first_kernel(where, a0, b0, g1, g2, g3, *outs):
-    spot = where[3]
-    logits = sum(r[:, D:].astype(F32) for r in (a0, b0, g1, g2, g3))
+def pair_kernel(shift, a, b, *refs):
+    total = a[:, D:].astype(F32) + b[:, D:].astype(F32)
+    if shift is None:
+        for i, out in enumerate(refs):
+            rows = slice(64 * i, 64 * (i + 1))
+            out[:, :D] = (a[rows, :D].astype(F32) + b[rows, :D].astype(F32)).astype(BF16)
+            out[:, D:] = split(joined(total[rows])).astype(BF16)
+        return
+    through, out = refs
+    for i in range(2):
+        rows = slice(64 * i, 64 * (i + 1))
+        part = a[rows, :D].astype(F32) + b[rows, :D].astype(F32)
+        logits = total[rows]
+        if i == shift:
+            part = part + through[:, :D].astype(F32)
+            logits = logits + through[:, D:].astype(F32)
+        out[rows, :D] = part.astype(BF16)
+        out[rows, D:] = split(joined(logits)).astype(BF16)
+
+
+def pair_sum(shift, *args):
+    outs = [((64, W), BF16)] * 2 if shift is None else [((128, W), BF16)]
+    kernel = functools.partial(pair_kernel, shift)
+    return small_call(kernel, "pair_sum", outs, *args, scalars=0)
+
+
+def first_kernel(where, a0, b0, g1, g3, *outs):
+    spot = where[5]
+    logits = sum(r[:, D:].astype(F32) for r in (a0, b0, g1, g3))
     logits = split(joined(logits)).astype(BF16)
     for d, out in enumerate(outs):
         rows = pl.ds(pl.multiple_of(lax.rem(spot + d, 4) * 32, 32), 32)
-        out[:, :D] = sum(r[rows, :D].astype(F32) for r in (a0, b0, g1, g2, g3)).astype(BF16)
+        out[:, :D] = sum(r[rows, :D].astype(F32) for r in (a0, b0, g1, g3)).astype(BF16)
         for k in range(4):
             out[:, D + 128 * k : D + 128 * (k + 1)] = logits[32 * k : 32 * (k + 1)]
 
 
 def second_kernel(where, m0, g1, g2, g3, *refs):
     outs, total, wide = refs[:4], refs[4], refs[5]
-    spot = where[4]
+    spot = where[6]
 
     def four(cols):
         a0, a1, a2, a3 = (r[:, cols].astype(F32) for r in (m0, g1, g2, g3))
@@ -257,6 +300,117 @@
     logits[...] = four(slice(D, W3))
 
 
+def collect_kernel(*refs):
+    for i, ref in enumerate(refs[:4]):
+        refs[4][i] = ref[...]
+
+
+def collect(parts):
+    shape = (4, *parts[0].shape)
+    return small_call(collect_kernel, "collect", [(shape, parts[0].dtype)], *parts, scalars=0)[0]
+
+
+def settle_kernel(source, target):
+    target[...] = source[...]
+
+
+def settle(value):
+    outs = [(value.shape, value.dtype)]
+    return small_call(settle_kernel, "settle", outs, value, scalars=0)[0]
+
+
+def halves_kernel(a, b, low, high):
+    low[...] = a[:2]
+    high[...] = b[2:]
+
+
+def halves(a, b):
+    shape = (2, *a.shape[1:])
+    outs = [(shape, a.dtype)] * 2
+    return small_call(halves_kernel, "halves", outs, a, b, scalars=0)
+
+
+def rows_kernel(where, block, side1, low, high, side3, out, wide):
+    core, x, y = where[0], where[1], where[2]
+    start = where[5] * 32 + where[6] * 8
+    even = pl.ds(pl.multiple_of(start // 16 * 16, 16), 16)
+    turn = lax.rem(y - x + 4, 4)
+
+    def put(j, value):
+        wide[...] = value.astype(F32)
+        rows = pl.ds(pl.multiple_of(lax.rem(start, 16), 8), 8)
+        out[:, pl.ds(pl.multiple_of(lax.rem(y + j, 4) * KB, 128), KB)] = wide[rows, :]
+
+    @pl.when(core == 0)
+    def _():
+        for j in range(4):
+            put(j, block[j, even, :])
+
+    @pl.when(core == 1)
+    def _():
+        put(0, block[turn, even, :])
+        put(1, side1[turn, even, :])
+        put(3, side3[turn, even, :])
+
+        @pl.when(turn < 2)
+        def _():
+            put(2, low[jnp.minimum(turn, 1), even, :])
+
+        @pl.when(turn >= 2)
+        def _():
+            put(2, high[jnp.maximum(turn - 2, 0), even, :])
+
+
+def finish_kernel(groups, where, own, oth, labels, bias, *refs):
+    actives, ya = refs[:4], refs[4]
+    grad, bias_grad, loss, logits, slopes = refs[5:]
+    core, x, y = where[0], where[1], where[2]
+    lane = lax.broadcasted_iota(jnp.int32, (8, 128), 1)
+
+    def unpack(source, start, parity):
+        for d in range(4):
+            g = lax.rem(start + d, 4) * 2 + parity
+            for i in range(8):
+                tile = source[d, :, 128 * i : 128 * (i + 1)]
+                logits[g, 8 * i : 8 * i + 8, :] = tile
+                logits[g, 64 + 8 * i : 72 + 8 * i, :] = pltpu.roll(tile, 64, 1)
+
+    @pl.when(core == 0)
+    def _():
+        unpack(own, x, 0)
+        unpack(oth, y, 1)
+
+    @pl.when(core == 1)
+    def _():
+        unpack(oth, x, 0)
+        unpack(own, y, 1)
+
+    slopes[...] = jnp.zeros_like(slopes)
+    total = jnp.zeros((128, 64), F32)
+    sums = jnp.zeros((1, 64), F32)
+    for g in range(groups):
+        value = logits[g, :, :64] + bias[...]
+        target = labels[128 * g : 128 * (g + 1), :].astype(F32)
+        slope = (jax.nn.sigmoid(value) - target).astype(BF16)
+        slopes[g, :, :64] = slope
+        total = total + (jax.nn.softplus(value) - target * value)
+        sums = sums + jnp.sum(slope.astype(F32), axis=0, keepdims=True)
+    loss[...] = jnp.broadcast_to(
+        jnp.sum(jnp.sum(total, axis=1, keepdims=True), axis=0, keepdims=True) / (groups * 128 * 64),
+        loss.shape,
+    )
+    bias_grad[...] = sums / 128
+
+    turned = jnp.zeros((128, ya.shape[2]), F32)
+    for d in range(4):
+        g = lax.rem(x + d, 4) * 2
+        for active, slope in ((actives[d][...], slopes[g]), (ya[d], slopes[g + 1])):
+            turned = turned + lax.dot_general(
+                slope, active, (((0,), (0,)), ((), ())), preferred_element_type=F32
+            )
+    grad[...] = (turned / 128)[:64]
+
+
 def on_device(
     residual, encoder, encoder_bias, thresholds, decoder, decoder_bias, probes, probe_bias, labels
 ):
@@ -269,16 +423,25 @@
     first = jnp.where(is0, x, y)
     second = jnp.where(is0, y, z)
     third = jnp.where(is0, z, x)
+    where = jnp.stack([core, x, y, z, first, second, third]).astype(jnp.int32)
+    probes2 = jnp.concatenate([probes, probes], axis=1)
 
     parts = [residual] + [pull(residual, "z", "z", d) for d in (1, 2, 3)]
     unit = absolute(parts, z).transpose(1, 0, 2).reshape(per_group, KB)
-    block = jnp.stack([unit] + [pull(unit, "y", "x", d) for d in (1, 2, 3)])
+    unit, where, probes2, encoder, decoder = lax.optimization_barrier(
+        (unit, where, probes2, encoder, decoder)
+    )
+    unit = settle(unit)
+    unit, encoder, decoder = lax.optimization_barrier((unit, encoder, decoder))
+    encoder, decoder = load(encoder), load(decoder)
+    pulled = [pull(unit, "y", "x", d) for d in (1, 2, 3)]
+    unit, pulled, encoder, decoder = lax.optimization_barrier((unit, pulled, encoder, decoder))
+    block = collect([unit, *pulled])
     own, oth = {0: [block]}, {0: [swap(block)]}
-    near = {d: pull(block, "x", "y", d) for d in (1, 3)}
-
-    cut = (thresholds.astype(F32) / levels)[None]
+    sides = {d: pull(block, "x", "y", d) for d in (1, 3)}
+
+    cut = thresholds[None]
     bias = encoder_bias[None]
-    where = jnp.stack([core, y]).astype(jnp.int32)
     xa = {}
 
     def run(stage, acc):
@@ -286,10 +449,11 @@
         return acc
 
     acc = run(0, None)
-    near, acc = lax.optimization_barrier((near, acc))
-    far = [pull(near[1][:2], "x", "y", 1), pull(near[3][2:], "x", "y", 3)]
+    sides, acc = lax.optimization_barrier((sides, acc))
+    low, high = halves(sides[1], sides[3])
+    far = [pull(low, "x", "y", 1), pull(high, "x", "y", 3)]
     for d in (1, 3):
-        own[d], oth[d] = [near[d]], [swap(near[d])]
+        own[d], oth[d] = [sides[d]], [swap(sides[d])]
     acc = run(1, acc)
     acc = run(3, acc)
     far, acc = lax.optimization_barrier((far, acc))
@@ -297,24 +461,33 @@
     acc = run(2, acc)
     ya = acc.reshape(4, 128, lat)
 
-    probes2 = jnp.concatenate([probes, probes], axis=1)
-    order = (2, 1, 3, 0)
-    keep, got, message = {}, {}, {}
-    for i, d in enumerate(order):
-        spot = jnp.stack([core, y, lax.rem(y + d - x + 4, 4)]).astype(jnp.int32)
-        left = xa[d]
-        if i >= 2:
-            left, message[order[i - 2]] = lax.optimization_barrier((left, message[order[i - 2]]))
-        keep[d], send = decode(spot, left, ya, decoder, probes2)
+    keep, got = {}, {}
+
+    def part(d, left):
+        keep[d], send = decode(d, where, left, ya, decoder, probes2)
         got[d] = swap(send)
-        if d:
-            message[d] = pair_sum(keep[d], got[d])
-    mine = {d: pull(message[d], "x", "y", 4 - d) for d in (2, 1, 3)}
-
-    where = jnp.stack([core, y, core, second, third]).astype(jnp.int32)
+
+    part(2, xa[2])
+    over = pair_sum(None, keep[2], got[2])
+    over, left0, left1 = lax.optimization_barrier((over, xa[0], xa[1]))
+    through = [pull(over[0], "x", "y", 3), pull(over[1], "x", "y", 1)]
+    part(0, left0)
+    part(1, left1)
+    through, keep[0], keep[1], left3 = lax.optimization_barrier(
+        (through, keep[0], keep[1], xa[3])
+    )
+    part(3, left3)
+    (message1,) = pair_sum(0, keep[1], got[1], through[0])
+    (message3,) = pair_sum(1, keep[3], got[3], through[1])
+    mine = {1: pull(message1, "x", "y", 3), 3: pull(message3, "x", "y", 1)}
+    (tokens,) = small_call(
+        rows_kernel, "own_rows", [((8, D), F32)],
+        where, block, sides[1], *far, sides[3], scratch=[pltpu.VMEM((16, KB), F32)],
+    )
+
     m2 = small_call(
         first_kernel, "first_sum", [((32, W2), BF16)] * 4,
-        where, keep[0], got[0], mine[1], mine[2], mine[3],
+        where, keep[0], got[0], mine[1], mine[3],
     )
     g2 = [pull(m2[d], "y", "z", 4 - d) for d in (1, 2, 3)]
     m3 = small_call(
@@ -322,21 +495,6 @@
         scratch=[pltpu.VMEM((32, D), F32), pltpu.VMEM((128, 128), F32)],
     )
     g3 = [pull(m3[d], "z", "x", 4 - d) for d in (1, 2, 3)]
-
-    start = second * 32 + third * 8
-    by_x = lax.dynamic_slice(block, (0, start, 0), (4, 8, KB))
-    turn = lax.rem(y - x + 4, 4)
-
-    def at(part, index):
-        return lax.dynamic_slice(part, (index, start, 0), (1, 8, KB))
-
-    low, high = at(far[0], jnp.minimum(turn, 1)), at(far[1], jnp.maximum(turn - 2, 0))
-    by_y = jnp.concatenate(
-        [at(block, turn), at(near[1], turn), jnp.where(turn < 2, low, high), at(near[3], turn)]
-    )
-    chosen = jnp.where(is0, by_x, by_y).astype(F32)
-    tokens = relative(chosen, lax.rem(4 - y, 4)).transpose(1, 0, 2).reshape(8, D)
-
     err, packed = small_call(
         third_kernel, "third_sum", [((8, 128), F32), ((8, 1024), F32)],
         m3[0], *g3, tokens, decoder_bias[None], scalars=0,
@@ -345,25 +503,17 @@
     for p, c in coords():
         s = (p["x"], p["y"], p["z"]) if c == 0 else (p["y"], p["z"], p["x"])
         owners.append((place(p, c), s[0] * 32 + c * 16 + s[1] * 4 + s[2]))
+
+    mine = collect([packed] + [pull(packed, "x", "y", d) for d in (1, 2, 3)])
+    theirs = swap(mine)
     error = lax.ppermute(err, AXES, owners)[:, 0]
-
-    mine = absolute([packed] + [pull(packed, "x", "y", d) for d in (1, 2, 3)], first)
-    theirs = swap(mine)
-    both = jnp.stack([jnp.where(is0, mine, theirs), jnp.where(is0, theirs, mine)], 1)
-    both = both.reshape(4, 2, 8, 8, 2, 64).transpose(0, 1, 4, 3, 2, 5).reshape(4, 2, 128, 64)
-    logits = both + probe_bias
-    target = labels.astype(F32).reshape(4, 2, 128, 64)
-    slopes = (jax.nn.sigmoid(logits) - target).astype(BF16)
-    mean_loss = jnp.sum(jax.nn.softplus(logits) - target * logits) / target.size
-    bias_grad = jnp.sum(slopes.astype(F32), axis=(0, 1, 2)) / per_group
-    turned = relative(slopes, x)
-    active = jnp.concatenate([xa[0], xa[1], xa[2], xa[3], ya.reshape(512, lat)])
-    turned = turned.transpose(1, 0, 2, 3).reshape(1024, 64)
-    probe_grad = (
-        lax.dot_general(active, turned, (((0,), (0,)), ((), ())), preferred_element_type=F32)
-        / per_group
-    )
-    return (error, probe_grad, bias_grad, mean_loss)
+    probe_grad, bias_grad, mean_loss = small_call(
+        functools.partial(finish_kernel, 8), "finish",
+        [((64, lat), F32), ((1, 64), F32), ((1, 128), F32)],
+        where, mine, theirs, labels, probe_bias[None], xa[0], xa[1], xa[2], xa[3], ya,
+        scratch=[pltpu.VMEM((8, 128, 128), F32), pltpu.VMEM((8, 128, 128), BF16)],
+    )
+    return (error, probe_grad.T, bias_grad[0], mean_loss[0, 0])
 
 
 def solution(mesh):

time: 175 us -> 158 us (0.903)
  local copies, waits for them, and re-layouts: 28.2 us -> 3.29 us
  waiting for transfers between devices: 51 us -> 60 us
  other arithmetic: 7.17 us -> 0.15 us
  starting transfers between devices: 36.7 us -> 43.3 us
  Pallas kernels: 46.7 us -> 50.1 us
  between operations: 3.04 us -> 1.02 us
    unnamed x83 -> x21, local copies, waits for them, and re-layouts: 22.6 us -> 2.31 us
    pallas_call x4 -> x6, Pallas kernels: 18.6 us -> 25.1 us  [the longest x4 17.5 us: decode(): pl.pallas_call(functools.partial(decode_kernel, step, 768), in_specs=[pl....]
    ppermute x22 -> x23, waiting for transfers between devices: 40.7 us -> 47.2 us  [pull(): return lax.ppermute(value, AXES, pull_perm(axis0, axis1, step))]
    ppermute x22 -> x23, starting transfers between devices: 30.5 us -> 36.8 us  [pull(): return lax.ppermute(value, AXES, pull_perm(axis0, axis1, step))]
    pallas_call x4, Pallas kernels: 20.4 us -> 17.1 us  [encode(): pl.pallas_call(functools.partial(encode_kernel, stage, len(own), 256), in...]
    ppermute x10, waiting for transfers between devices: 2.94 us -> 5.73 us  [swap(): return lax.ppermute(value, AXES, pairs)]
    slice x2 -> x0, local copies, waits for them, and re-layouts: 2.22 us -> none  [on_device(): far = [pull(near[1][:2], 'x', 'y', 1), pull(near[3][2:], 'x', 'y', 3)]]
    convert_element_type x2 -> x0, other arithmetic: 2.02 us -> none  [the longest x1 1.87 us: on_device(): target = labels.astype(F32).reshape(4, 2, 128, 64)]
  transfers between devices with their start and end apart: 33 -> 34, of which waited for: 19 -> 20; matrix products, arithmetic and copies ran while one was open for 7% -> 2% of each run, Pallas kernels for 18% -> 22%
where the time goes in v2:
time: 158 us
  waiting for transfers between devices  60 us (38%)
  Pallas kernels  50.1 us (32%)
  starting transfers between devices  43.3 us (27%)
  local copies, waits for them, and re-layouts  3.29 us (2%)
    ppermute x23, waiting for transfers between devices, pull(): return lax.ppermute(value, AXES, pull_perm(axis0, axis1, step))  47.2 us
    ppermute x23, starting transfers between devices, pull(): return lax.ppermute(value, AXES, pull_perm(axis0, axis1, step))  36.8 us
    pallas_call x4, Pallas kernels, decode(): pl.pallas_call(functools.partial(decode_kernel, step, 768), in_specs=[pl....  17.5 us
    pallas_call x4, Pallas kernels, encode(): pl.pallas_call(functools.partial(encode_kernel, stage, len(own), 256), in...  17.1 us
    pallas_call x12, Pallas kernels, small_call(): pl.pallas_call(kernel, in_specs=[smem] * scalars + [vmem] * (len(args) -...  7.95 us
    pallas_call x2, Pallas kernels, load(): pl.pallas_call(load_kernel, in_specs=[pl.BlockSpec(memory_space=pltpu.HBM...  7.6 us
    ppermute x1, waiting for transfers between devices, on_device(): error = lax.ppermute(err, AXES, owners)[:, 0]  7.14 us
    ppermute x10, waiting for transfers between devices, swap(): return lax.ppermute(value, AXES, pairs)  5.73 us
  transfers between devices with their start and end apart: 34, of which 20 were waited for; matrix products, arithmetic and copies ran while one was open for 2% of the time, Pallas kernels for 22%

profile of v2, /device:TPU:26, one launch (start us, length us, event | category | flops | bytes accessed | tf_op | source)
XLA Modules:
  0.0 157.9 jit_solution(10727979333788474545)
XLA Ops:
  0.6 4.1 %collective-permute-start = (bf16[128,288]{0,1:T(8,128)(2,1)}, bf16[128,288]{0,1:T(8,128)(2,1)S(1)}, u32[]{:S(2)}, u32[]{:S(2)}) collective-permute-start(bf16[128,288]{0,1:T(8,128)(2,1)} %param.9), channel_id=1, source_target_pairs={{8,0},{9,1},{10,2},{11,3},{12,4},{13,5},{14,6},{15,7},{16,8},{17,9... | collective-permute-start | bytes 221192 | tf_op jit(solution)/shard_map/ppermute | solution.py:51
  8.3 2.7 %collective-permute-done.1 = bf16[128,288]{0,1:T(8,128)(2,1)S(1)} collective-permute-done((bf16[128,288]{0,1:T(8,128)(2,1)}, bf16[128,288]{0,1:T(8,128)(2,1)S(1)}, u32[]{:S(2)}, u32[]{:S(2)}) %collective-permute-start.1) | collective-permute-done | bytes 73760 | tf_op jit(solution)/shard_map/ppermute | solution.py:51
  13.6 2.2 %collective-permute-start.5 = (bf16[128,1152]{1,0:T(8,128)(2,1)S(1)}, bf16[128,1152]{1,0:T(8,128)(2,1)S(1)}, u32[]{:S(2)}, u32[]{:S(2)}) collective-permute-start(bf16[128,1152]{1,0:T(8,128)(2,1)S(1)} %settle.1.refs_0_), channel_id=1, source_target_pairs={{96,0},{7,1},{98,2},{1,3},{100,4},{3,5},{102,6},{5,7},{104,8},{15,... | collective-permute-start | bytes 884744 | tf_op jit(solution)/shard_map/ppermute | solution.py:51
  15.8 3.8 %load.2.refs_2_.refs_4_ = bf16[4608,1024]{1,0:T(8,128)(2,1)S(1)} custom-call(bf16[4608,1024]{1,0:T(8,128)(2,1)} %source), custom_call_target="tpu_custom_call" | custom-call | flops 1000000 | tf_op jit(solution)/shard_map/load/pallas_call | solution.py:78
  19.6 3.8 %load.3.dec = bf16[1024,4608]{1,0:T(8,128)(2,1)S(1)} custom-call(bf16[1024,4608]{1,0:T(8,128)(2,1)} %source.1), custom_call_target="tpu_custom_call" | custom-call | flops 1000000 | tf_op jit(solution)/shard_map/load/pallas_call | solution.py:78
  26.9 4.1 %encode.4 = (bf16[128,1024]{1,0:T(8,128)(2,1)S(1)}, f32[512,1024]{1,0:T(8,128)S(1)}) custom-call(s32[7]{0:T(128)S(1)} %stack.55.where, bf16[4,128,1152]{2,1,0:T(8,128)(2,1)S(1)} %collect.2.refs_0_.block, bf16[4,128,1152]{2,1,0:T(8,128)(2,1)S(1)} %collective-permute-done.8.refs_1_, bf16[4608,1024]{1,0:T(8,128)(2,1)S(1)} %load.2.refs_2_.refs_4_, ...), custom_call_target="tpu_custom_call" | custom-call | flops 1000000 | tf_op jit(solution)/shard_map/encode/pallas_call | solution.py:159
  31.1 9.3 %collective-permute-done.6.a.refs_0_.side1 = bf16[4,128,1152]{2,1,0:T(8,128)(2,1)S(1)} collective-permute-done((bf16[4,128,1152]{2,1,0:T(8,128)(2,1)S(1)}, bf16[4,128,1152]{2,1,0:T(8,128)(2,1)S(1)}, u32[]{:S(2)}, u32[]{:S(2)}) %collective-permute-start.6) | collective-permute-done | bytes 1179680 | tf_op jit(solution)/shard_map/ppermute | solution.py:51
  43.1 2.6 %collective-permute-start.9 = (bf16[2,128,1152]{2,1,0:T(8,128)(2,1)S(1)}, bf16[2,128,1152]{2,1,0:T(8,128)(2,1)S(1)}, u32[]{:S(2)}, u32[]{:S(2)}) collective-permute-start(bf16[2,128,1152]{2,1,0:T(8,128)(2,1)S(1)} %get-tuple-element.81), channel_id=1, source_target_pairs={{2,0},{33,1},{4,2},{35,3},{6,4},{37,5},{0,6},{39,7},{10,8},{41,9},... | collective-permute-start | bytes 1769480 | tf_op jit(solution)/shard_map/ppermute | solution.py:51
  45.6 4.2 %encode.5 = (bf16[128,1024]{1,0:T(8,128)(2,1)S(1)}, f32[512,1024]{1,0:T(8,128)S(1)}) custom-call(s32[7]{0:T(128)S(1)} %stack.55.where, bf16[4,128,1152]{2,1,0:T(8,128)(2,1)S(1)} %collective-permute-done.6.a.refs_0_.side1, bf16[4,128,1152]{2,1,0:T(8,128)(2,1)S(1)} %collective-permute-done.12.refs_1_, ...), custom_call_target="tpu_custom_call", output_to_operand_aliasing={{1}: (6, {})} | custom-call | flops 1000000 | tf_op jit(solution)/shard_map/encode/pallas_call | solution.py:159
  49.8 4.2 %encode.6 = (bf16[128,1024]{1,0:T(8,128)(2,1)S(1)}, f32[512,1024]{1,0:T(8,128)S(1)}) custom-call(s32[7]{0:T(128)S(1)} %stack.55.where, bf16[4,128,1152]{2,1,0:T(8,128)(2,1)S(1)} %collective-permute-done.7.b.refs_0_.side3, bf16[4,128,1152]{2,1,0:T(8,128)(2,1)S(1)} %collective-permute-done.11.refs_1_, ...), custom_call_target="tpu_custom_call", output_to_operand_aliasing={{1}: (6, {})} | custom-call | flops 1000000 | tf_op jit(solution)/shard_map/encode/pallas_call | solution.py:159
  57.1 4.6 %encode.7 = (bf16[128,1024]{1,0:T(8,128)(2,1)S(1)}, bf16[512,1024]{1,0:T(8,128)(2,1)S(1)}) custom-call(s32[7]{0:T(128)S(1)} %stack.55.where, bf16[2,128,1152]{2,1,0:T(8,128)(2,1)S(1)} %collective-permute-done.9.refs_0_.low, bf16[2,128,1152]{2,1,0:T(8,128)(2,1)S(1)} %collective-permute-done.10.refs_1_.high, ...), custom_call_target="tpu_custom_call" | custom-call | flops 1000000 | tf_op jit(solution)/shard_map/encode/pallas_call | solution.py:159
  61.7 4.4 %decode.4 = (bf16[128,4736]{1,0:T(8,128)(2,1)S(1)}, bf16[128,4736]{1,0:T(8,128)(2,1)S(1)}) custom-call(s32[7]{0:T(128)S(1)} %stack.55.where, bf16[128,1024]{1,0:T(8,128)(2,1)S(1)} %get-tuple-element.89.xa.refs_2_, bf16[4,128,1024]{2,1,0:T(8,128)(2,1)S(1)} %bitcast.30, bf16[1024,4608]{1,0:T(8,128)(2,1)S(1)} %load.3.dec, ...), custom_call_target="tpu_custom_call" | custom-call | flops 1000000 | tf_op jit(solution)/shard_map/decode/pallas_call | solution.py:204
  66.5 2.5 %collective-permute-done.15.b = bf16[128,4736]{1,0:T(8,128)(2,1)S(1)} collective-permute-done((bf16[128,4736]{1,0:T(8,128)(2,1)S(1)}, bf16[128,4736]{1,0:T(8,128)(2,1)S(1)}, u32[]{:S(2)}, u32[]{:S(2)}) %collective-permute-start.15) | collective-permute-done | bytes 1212448 | tf_op jit(solution)/shard_map/ppermute | solution.py:56
  69.6 1.9 %collective-permute-start.16 = (bf16[64,4736]{1,0:T(8,128)(2,1)S(1)}, bf16[64,4736]{1,0:T(8,128)(2,1)S(1)}, u32[]{:S(2)}, u32[]{:S(2)}) collective-permute-start(bf16[64,4736]{1,0:T(8,128)(2,1)S(1)} %get-tuple-element.99), channel_id=1, source_target_pairs={{6,0},{97,1},{0,2},{99,3},{2,4},{101,5},{4,6},{103,7},{14,8},{105,... | collective-permute-start | bytes 1818632 | tf_op jit(solution)/shard_map/ppermute | solution.py:51
  73.0 4.4 %decode.6 = (bf16[128,4736]{1,0:T(8,128)(2,1)S(1)}, bf16[128,4736]{1,0:T(8,128)(2,1)S(1)}) custom-call(s32[7]{0:T(128)S(1)} %stack.55.where, bf16[128,1024]{1,0:T(8,128)(2,1)S(1)} %get-tuple-element.103.xa.refs_1_, bf16[4,128,1024]{2,1,0:T(8,128)(2,1)S(1)} %bitcast.31, bf16[1024,4608]{1,0:T(8,128)(2,1)S(1)} %load.3.dec, ...), custom_call_target="tpu_custom_call" | custom-call | flops 1000000 | tf_op jit(solution)/shard_map/decode/pallas_call | solution.py:204
  77.5 4.4 %decode.5 = (bf16[128,4736]{1,0:T(8,128)(2,1)S(1)}, bf16[128,4736]{1,0:T(8,128)(2,1)S(1)}) custom-call(s32[7]{0:T(128)S(1)} %stack.55.where, bf16[128,1024]{1,0:T(8,128)(2,1)S(1)} %get-tuple-element.101.xa.refs_0_, bf16[4,128,1024]{2,1,0:T(8,128)(2,1)S(1)} %bitcast.32, bf16[1024,4608]{1,0:T(8,128)(2,1)S(1)} %load.3.dec, ...), custom_call_target="tpu_custom_call" | custom-call | flops 1000000 | tf_op jit(solution)/shard_map/decode/pallas_call | solution.py:204
  82.8 4.4 %decode.7 = (bf16[128,4736]{1,0:T(8,128)(2,1)S(1)}, bf16[128,4736]{1,0:T(8,128)(2,1)S(1)}) custom-call(s32[7]{0:T(128)S(1)} %stack.55.where, bf16[128,1024]{1,0:T(8,128)(2,1)S(1)} %get-tuple-element.111.xa.refs_3_, bf16[4,128,1024]{2,1,0:T(8,128)(2,1)S(1)} %bitcast.33, bf16[1024,4608]{1,0:T(8,128)(2,1)S(1)} %load.3.dec, ...), custom_call_target="tpu_custom_call" | custom-call | flops 1000000 | tf_op jit(solution)/shard_map/decode/pallas_call | solution.py:204
  88.5 2.1 %collective-permute-start.20 = (bf16[128,4736]{1,0:T(8,128)(2,1)S(1)}, bf16[128,4736]{1,0:T(8,128)(2,1)S(1)}, u32[]{:S(2)}, u32[]{:S(2)}) collective-permute-start(bf16[128,4736]{1,0:T(8,128)(2,1)S(1)} %pair_sum.4), channel_id=1, source_target_pairs={{6,0},{97,1},{0,2},{99,3},{2,4},{101,5},{4,6},{103,7},{14,8},{105,... | collective-permute-start | bytes 3637256 | tf_op jit(solution)/shard_map/ppermute | solution.py:51
  91.3 2.0 %collective-permute-start.22 = (bf16[128,4736]{1,0:T(8,128)(2,1)S(1)}, bf16[128,4736]{1,0:T(8,128)(2,1)S(1)}, u32[]{:S(2)}, u32[]{:S(2)}) collective-permute-start(bf16[128,4736]{1,0:T(8,128)(2,1)S(1)} %pair_sum.5), channel_id=1, source_target_pairs={{2,0},{33,1},{4,2},{35,3},{6,4},{37,5},{0,6},{39,7},{10,8},{41,9},... | collective-permute-start | bytes 3637256 | tf_op jit(solution)/shard_map/ppermute | solution.py:51
  93.3 12.1 %collective-permute-done.20.g1 = bf16[128,4736]{1,0:T(8,128)(2,1)S(1)} collective-permute-done((bf16[128,4736]{1,0:T(8,128)(2,1)S(1)}, bf16[128,4736]{1,0:T(8,128)(2,1)S(1)}, u32[]{:S(2)}, u32[]{:S(2)}) %collective-permute-start.20) | collective-permute-done | bytes 1212448 | tf_op jit(solution)/shard_map/ppermute | solution.py:51
  105.5 2.6 %collective-permute-done.22.g3 = bf16[128,4736]{1,0:T(8,128)(2,1)S(1)} collective-permute-done((bf16[128,4736]{1,0:T(8,128)(2,1)S(1)}, bf16[128,4736]{1,0:T(8,128)(2,1)S(1)}, u32[]{:S(2)}, u32[]{:S(2)}) %collective-permute-start.22) | collective-permute-done | bytes 1212448 | tf_op jit(solution)/shard_map/ppermute | solution.py:51
  109.7 2.6 %collective-permute-start.23 = (bf16[32,5120]{1,0:T(8,128)(2,1)S(1)}, bf16[32,5120]{1,0:T(8,128)(2,1)S(1)}, u32[]{:S(2)}, u32[]{:S(2)}) collective-permute-start(bf16[32,5120]{1,0:T(8,128)(2,1)S(1)} %get-tuple-element.116), channel_id=1, source_target_pairs={{96,0},{25,1},{98,2},{27,3},{100,4},{29,5},{102,6},{31,7},{104,8},... | collective-permute-start | bytes 983048 | tf_op jit(solution)/shard_map/ppermute | solution.py:51
  113.3 7.2 %collective-permute-done.23.g1 = bf16[32,5120]{1,0:T(8,128)(2,1)S(1)} collective-permute-done((bf16[32,5120]{1,0:T(8,128)(2,1)S(1)}, bf16[32,5120]{1,0:T(8,128)(2,1)S(1)}, u32[]{:S(2)}, u32[]{:S(2)}) %collective-permute-start.23) | collective-permute-done | bytes 327712 | tf_op jit(solution)/shard_map/ppermute | solution.py:51
  121.0 3.1 %collective-permute-done.25.g3 = bf16[32,5120]{1,0:T(8,128)(2,1)S(1)} collective-permute-done((bf16[32,5120]{1,0:T(8,128)(2,1)S(1)}, bf16[32,5120]{1,0:T(8,128)(2,1)S(1)}, u32[]{:S(2)}, u32[]{:S(2)}) %collective-permute-start.25) | collective-permute-done | bytes 327712 | tf_op jit(solution)/shard_map/ppermute | solution.py:51
  125.1 2.3 %collective-permute-start.27 = (f32[8,5632]{1,0:T(8,128)S(1)}, f32[8,5632]{1,0:T(8,128)S(1)}, u32[]{:S(2)}, u32[]{:S(2)}) collective-permute-start(f32[8,5632]{1,0:T(8,128)S(1)} %get-tuple-element.121), channel_id=1, source_target_pairs={{16,0},{5,1},{18,2},{7,3},{20,4},{1,5},{22,6},{3,7},{24,8},{13,9},... | collective-permute-start | bytes 540680 | tf_op jit(solution)/shard_map/ppermute | solution.py:51
  129.8 4.0 %collective-permute-done.26.g1 = f32[8,5632]{1,0:T(8,128)S(1)} collective-permute-done((f32[8,5632]{1,0:T(8,128)S(1)}, f32[8,5632]{1,0:T(8,128)S(1)}, u32[]{:S(2)}, u32[]{:S(2)}) %collective-permute-start.26) | collective-permute-done | bytes 180256 | tf_op jit(solution)/shard_map/ppermute | solution.py:51
  134.7 1.9 %collective-permute-start.30 = (f32[8,1024]{1,0:T(8,128)S(1)}, f32[8,1024]{1,0:T(8,128)S(1)}, u32[]{:S(2)}, u32[]{:S(2)}) collective-permute-start(f32[8,1024]{1,0:T(8,128)S(1)} %get-tuple-element.124.refs_0_), channel_id=1, source_target_pairs={{2,0},{33,1},{4,2},{35,3},{6,4},{37,5},{0,6},{39,7},{10,8},{41,9},... | collective-permute-start | bytes 98312 | tf_op jit(solution)/shard_map/ppermute | solution.py:51
  136.7 2.4 %collective-permute-start.31 = (f32[8,1024]{1,0:T(8,128)S(1)}, f32[8,1024]{1,0:T(8,128)S(1)}, u32[]{:S(2)}, u32[]{:S(2)}) collective-permute-start(f32[8,1024]{1,0:T(8,128)S(1)} %get-tuple-element.124.refs_0_), channel_id=1, source_target_pairs={{4,0},{65,1},{6,2},{67,3},{0,4},{69,5},{2,6},{71,7},{12,8},{73,9},... | collective-permute-start | bytes 98312 | tf_op jit(solution)/shard_map/ppermute | solution.py:51
  139.1 2.5 %collective-permute-start.32 = (f32[8,1024]{1,0:T(8,128)S(1)}, f32[8,1024]{1,0:T(8,128)S(1)}, u32[]{:S(2)}, u32[]{:S(2)}) collective-permute-start(f32[8,1024]{1,0:T(8,128)S(1)} %get-tuple-element.124.refs_0_), channel_id=1, source_target_pairs={{6,0},{97,1},{0,2},{99,3},{2,4},{101,5},{4,6},{103,7},{14,8},{105,... | collective-permute-start | bytes 98312 | tf_op jit(solution)/shard_map/ppermute | solution.py:51
  143.3 4.2 %collective-permute-start.29 = (f32[8,128]{1,0:T(8,128)S(1)}, f32[8,128]{1,0:T(8,128)S(1)}, u32[]{:S(2)}, u32[]{:S(2)}) collective-permute-start(f32[8,128]{1,0:T(8,128)S(1)} %get-tuple-element.123), channel_id=1, source_target_pairs={{0,0},{1,16},{2,32},{3,17},{4,64},{5,18},{6,96},{7,19},{8,1},{9,20... | collective-permute-start | bytes 12296 | tf_op jit(solution)/shard_map/ppermute | solution.py:509
  147.7 7.1 %collective-permute-done.29 = f32[8,128]{1,0:T(8,128)S(1)} collective-permute-done((f32[8,128]{1,0:T(8,128)S(1)}, f32[8,128]{1,0:T(8,128)S(1)}, u32[]{:S(2)}, u32[]{:S(2)}) %collective-permute-start.29) | collective-permute-done | bytes 4128 | tf_op jit(solution)/shard_map/ppermute | solution.py:509
  155.5 2.4 %finish.1 = (f32[64,1024]{1,0:T(8,128)}, f32[1,64]{1,0:T(1,128)}, f32[1,128]{1,0:T(1,128)}) custom-call(s32[7]{0:T(128)S(1)} %stack.55.where, f32[4,8,1024]{2,1,0:T(8,128)S(1)} %collect.3.own, f32[4,8,1024]{2,1,0:T(8,128)S(1)} %collective-permute-done.33.oth, s32[1024,64]{1,0:T(8,128)S(1)} %copy.22.labels, f32[1,64]{1,0:T(1,128)S(1)} %bitcast.43, ...), custom_call_target="tpu_custom_call" | custom-call | flops 1000000 | tf_op jit(solution)/shard_map/finish/pallas_call | solution.py:219
  (86 shorter events, 30.8 us)
Async XLA Ops:
  0.6 7.6 %collective-permute-start = (bf16[128,288]{0,1:T(8,128)(2,1)}, bf16[128,288]{0,1:T(8,128)(2,1)S(1)}, u32[]{:S(2)}, u32[]{:S(2)}) collective-permute-start(bf16[128,288]{0,1:T(8,128)(2,1)} %param.9), channel_id=1, source_target_pairs={{8,0},{9,1},{10,2},{11,3},{12,4},{13,5},{14,6},{15,7},{16,8},{17,9... | collective-permute-start | bytes 221192 | tf_op jit(solution)/shard_map/ppermute | solution.py:51
  4.7 6.3 %collective-permute-start.1 = (bf16[128,288]{0,1:T(8,128)(2,1)}, bf16[128,288]{0,1:T(8,128)(2,1)S(1)}, u32[]{:S(2)}, u32[]{:S(2)}) collective-permute-start(bf16[128,288]{0,1:T(8,128)(2,1)} %param.9), channel_id=1, source_target_pairs={{16,0},{17,1},{18,2},{19,3},{20,4},{21,5},{22,6},{23,7},{24,8},{25... | collective-permute-start | bytes 221192 | tf_op jit(solution)/shard_map/ppermute | solution.py:51
  4.7 6.7 %collective-permute-start.2 = (bf16[128,288]{0,1:T(8,128)(2,1)}, bf16[128,288]{0,1:T(8,128)(2,1)S(1)}, u32[]{:S(2)}, u32[]{:S(2)}) collective-permute-start(bf16[128,288]{0,1:T(8,128)(2,1)} %param.9), channel_id=1, source_target_pairs={{24,0},{25,1},{26,2},{27,3},{28,4},{29,5},{30,6},{31,7},{0,8},{1,9... | collective-permute-start | bytes 221192 | tf_op jit(solution)/shard_map/ppermute | solution.py:51
  11.9 11.6 %collective-permute-start.3 = (bf16[128,1152]{1,0:T(8,128)(2,1)S(1)}, bf16[128,1152]{1,0:T(8,128)(2,1)S(1)}, u32[]{:S(2)}, u32[]{:S(2)}) collective-permute-start(bf16[128,1152]{1,0:T(8,128)(2,1)S(1)} %settle.1.refs_0_), channel_id=1, source_target_pairs={{32,0},{3,1},{34,2},{5,3},{36,4},{7,5},{38,6},{1,7},{40,8},{11,9},... | collective-permute-start | bytes 884744 | tf_op jit(solution)/shard_map/ppermute | solution.py:51
  12.7 10.8 %collective-permute-start.4 = (bf16[128,1152]{1,0:T(8,128)(2,1)S(1)}, bf16[128,1152]{1,0:T(8,128)(2,1)S(1)}, u32[]{:S(2)}, u32[]{:S(2)}) collective-permute-start(bf16[128,1152]{1,0:T(8,128)(2,1)S(1)} %settle.1.refs_0_), channel_id=1, source_target_pairs={{64,0},{5,1},{66,2},{7,3},{68,4},{1,5},{70,6},{3,7},{72,8},{13,9},... | collective-permute-start | bytes 884744 | tf_op jit(solution)/shard_map/ppermute | solution.py:51
  13.6 10.3 %collective-permute-start.5 = (bf16[128,1152]{1,0:T(8,128)(2,1)S(1)}, bf16[128,1152]{1,0:T(8,128)(2,1)S(1)}, u32[]{:S(2)}, u32[]{:S(2)}) collective-permute-start(bf16[128,1152]{1,0:T(8,128)(2,1)S(1)} %settle.1.refs_0_), channel_id=1, source_target_pairs={{96,0},{7,1},{98,2},{1,3},{100,4},{3,5},{102,6},{5,7},{104,8},{15,... | collective-permute-start | bytes 884744 | tf_op jit(solution)/shard_map/ppermute | solution.py:51
  24.0 2.9 %collective-permute-start.8 = (bf16[4,128,1152]{2,1,0:T(8,128)(2,1)S(1)}, bf16[4,128,1152]{2,1,0:T(8,128)(2,1)S(1)}, u32[]{:S(2)}, u32[]{:S(2)}) collective-permute-start(bf16[4,128,1152]{2,1,0:T(8,128)(2,1)S(1)} %collect.2.refs_0_.block), channel_id=1, source_target_pairs={{0,1},{1,0},{2,3},{3,2},{4,5},{5,4},{6,7},{7,6},{8,9},{9,8},{10,11... | collective-permute-start | bytes 3538952 | tf_op jit(solution)/shard_map/ppermute | solution.py:56
  24.1 16.3 %collective-permute-start.6 = (bf16[4,128,1152]{2,1,0:T(8,128)(2,1)S(1)}, bf16[4,128,1152]{2,1,0:T(8,128)(2,1)S(1)}, u32[]{:S(2)}, u32[]{:S(2)}) collective-permute-start(bf16[4,128,1152]{2,1,0:T(8,128)(2,1)S(1)} %collect.2.refs_0_.block), channel_id=1, source_target_pairs={{2,0},{33,1},{4,2},{35,3},{6,4},{37,5},{0,6},{39,7},{10,8},{41,9},... | collective-permute-start | bytes 3538952 | tf_op jit(solution)/shard_map/ppermute | solution.py:51
  24.7 16.9 %collective-permute-start.7 = (bf16[4,128,1152]{2,1,0:T(8,128)(2,1)S(1)}, bf16[4,128,1152]{2,1,0:T(8,128)(2,1)S(1)}, u32[]{:S(2)}, u32[]{:S(2)}) collective-permute-start(bf16[4,128,1152]{2,1,0:T(8,128)(2,1)S(1)} %collect.2.refs_0_.block), channel_id=1, source_target_pairs={{6,0},{97,1},{0,2},{99,3},{2,4},{101,5},{4,6},{103,7},{14,8},{105,... | collective-permute-start | bytes 3538952 | tf_op jit(solution)/shard_map/ppermute | solution.py:51
  41.6 4.0 %collective-permute-start.12 = (bf16[4,128,1152]{2,1,0:T(8,128)(2,1)S(1)}, bf16[4,128,1152]{2,1,0:T(8,128)(2,1)S(1)}, u32[]{:S(2)}, u32[]{:S(2)}) collective-permute-start(bf16[4,128,1152]{2,1,0:T(8,128)(2,1)S(1)} %collective-permute-done.6.a.refs_0_.side1), channel_id=1, source_target_pairs={{0,1},{1,0},{2,3},{3,2},{4,5},{5,4},{6,7},{7,6},{8,9},{9,8},{10,11... | collective-permute-start | bytes 3538952 | tf_op jit(solution)/shard_map/ppermute | solution.py:56
  41.6 8.2 %collective-permute-start.11 = (bf16[4,128,1152]{2,1,0:T(8,128)(2,1)S(1)}, bf16[4,128,1152]{2,1,0:T(8,128)(2,1)S(1)}, u32[]{:S(2)}, u32[]{:S(2)}) collective-permute-start(bf16[4,128,1152]{2,1,0:T(8,128)(2,1)S(1)} %collective-permute-done.7.b.refs_0_.side3), channel_id=1, source_target_pairs={{0,1},{1,0},{2,3},{3,2},{4,5},{5,4},{6,7},{7,6},{8,9},{9,8},{10,11... | collective-permute-start | bytes 3538952 | tf_op jit(solution)/shard_map/ppermute | solution.py:56
  42.2 11.8 %collective-permute-start.10 = (bf16[2,128,1152]{2,1,0:T(8,128)(2,1)S(1)}, bf16[2,128,1152]{2,1,0:T(8,128)(2,1)S(1)}, u32[]{:S(2)}, u32[]{:S(2)}) collective-permute-start(bf16[2,128,1152]{2,1,0:T(8,128)(2,1)S(1)} %get-tuple-element.82), channel_id=1, source_target_pairs={{6,0},{97,1},{0,2},{99,3},{2,4},{101,5},{4,6},{103,7},{14,8},{105,... | collective-permute-start | bytes 1769480 | tf_op jit(solution)/shard_map/ppermute | solution.py:51
  43.1 11.0 %collective-permute-start.9 = (bf16[2,128,1152]{2,1,0:T(8,128)(2,1)S(1)}, bf16[2,128,1152]{2,1,0:T(8,128)(2,1)S(1)}, u32[]{:S(2)}, u32[]{:S(2)}) collective-permute-start(bf16[2,128,1152]{2,1,0:T(8,128)(2,1)S(1)} %get-tuple-element.81), channel_id=1, source_target_pairs={{2,0},{33,1},{4,2},{35,3},{6,4},{37,5},{0,6},{39,7},{10,8},{41,9},... | collective-permute-start | bytes 1769480 | tf_op jit(solution)/shard_map/ppermute | solution.py:51
  66.1 3.0 %collective-permute-start.15 = (bf16[128,4736]{1,0:T(8,128)(2,1)S(1)}, bf16[128,4736]{1,0:T(8,128)(2,1)S(1)}, u32[]{:S(2)}, u32[]{:S(2)}) collective-permute-start(bf16[128,4736]{1,0:T(8,128)(2,1)S(1)} %get-tuple-element.94), channel_id=1, source_target_pairs={{0,1},{1,0},{2,3},{3,2},{4,5},{5,4},{6,7},{7,6},{8,9},{9,8},{10,11... | collective-permute-start | bytes 3637256 | tf_op jit(solution)/shard_map/ppermute | solution.py:56
  69.6 12.2 %collective-permute-start.16 = (bf16[64,4736]{1,0:T(8,128)(2,1)S(1)}, bf16[64,4736]{1,0:T(8,128)(2,1)S(1)}, u32[]{:S(2)}, u32[]{:S(2)}) collective-permute-start(bf16[64,4736]{1,0:T(8,128)(2,1)S(1)} %get-tuple-element.99), channel_id=1, source_target_pairs={{6,0},{97,1},{0,2},{99,3},{2,4},{101,5},{4,6},{103,7},{14,8},{105,... | collective-permute-start | bytes 1818632 | tf_op jit(solution)/shard_map/ppermute | solution.py:51
  71.5 11.3 %collective-permute-start.17 = (bf16[64,4736]{1,0:T(8,128)(2,1)S(1)}, bf16[64,4736]{1,0:T(8,128)(2,1)S(1)}, u32[]{:S(2)}, u32[]{:S(2)}) collective-permute-start(bf16[64,4736]{1,0:T(8,128)(2,1)S(1)} %get-tuple-element.100), channel_id=1, source_target_pairs={{2,0},{33,1},{4,2},{35,3},{6,4},{37,5},{0,6},{39,7},{10,8},{41,9},... | collective-permute-start | bytes 1818632 | tf_op jit(solution)/shard_map/ppermute | solution.py:51
  77.4 10.3 %collective-permute-start.19 = (bf16[128,4736]{1,0:T(8,128)(2,1)S(1)}, bf16[128,4736]{1,0:T(8,128)(2,1)S(1)}, u32[]{:S(2)}, u32[]{:S(2)}) collective-permute-start(bf16[128,4736]{1,0:T(8,128)(2,1)S(1)} %get-tuple-element.109), channel_id=1, source_target_pairs={{0,1},{1,0},{2,3},{3,2},{4,5},{5,4},{6,7},{7,6},{8,9},{9,8},{10,11... | collective-permute-start | bytes 3637256 | tf_op jit(solution)/shard_map/ppermute | solution.py:56
  87.2 3.4 %collective-permute-start.21 = (bf16[128,4736]{1,0:T(8,128)(2,1)S(1)}, bf16[128,4736]{1,0:T(8,128)(2,1)S(1)}, u32[]{:S(2)}, u32[]{:S(2)}) collective-permute-start(bf16[128,4736]{1,0:T(8,128)(2,1)S(1)} %get-tuple-element.113), channel_id=1, source_target_pairs={{0,1},{1,0},{2,3},{3,2},{4,5},{5,4},{6,7},{7,6},{8,9},{9,8},{10,11... | collective-permute-start | bytes 3637256 | tf_op jit(solution)/shard_map/ppermute | solution.py:56
  87.3 6.1 %collective-permute-start.18 = (bf16[128,4736]{1,0:T(8,128)(2,1)S(1)}, bf16[128,4736]{1,0:T(8,128)(2,1)S(1)}, u32[]{:S(2)}, u32[]{:S(2)}) collective-permute-start(bf16[128,4736]{1,0:T(8,128)(2,1)S(1)} %get-tuple-element.107), channel_id=1, source_target_pairs={{0,1},{1,0},{2,3},{3,2},{4,5},{5,4},{6,7},{7,6},{8,9},{9,8},{10,11... | collective-permute-start | bytes 3637256 | tf_op jit(solution)/shard_map/ppermute | solution.py:56
  88.5 17.0 %collective-permute-start.20 = (bf16[128,4736]{1,0:T(8,128)(2,1)S(1)}, bf16[128,4736]{1,0:T(8,128)(2,1)S(1)}, u32[]{:S(2)}, u32[]{:S(2)}) collective-permute-start(bf16[128,4736]{1,0:T(8,128)(2,1)S(1)} %pair_sum.4), channel_id=1, source_target_pairs={{6,0},{97,1},{0,2},{99,3},{2,4},{101,5},{4,6},{103,7},{14,8},{105,... | collective-permute-start | bytes 3637256 | tf_op jit(solution)/shard_map/ppermute | solution.py:51
  91.3 16.7 %collective-permute-start.22 = (bf16[128,4736]{1,0:T(8,128)(2,1)S(1)}, bf16[128,4736]{1,0:T(8,128)(2,1)S(1)}, u32[]{:S(2)}, u32[]{:S(2)}) collective-permute-start(bf16[128,4736]{1,0:T(8,128)(2,1)S(1)} %pair_sum.5), channel_id=1, source_target_pairs={{2,0},{33,1},{4,2},{35,3},{6,4},{37,5},{0,6},{39,7},{10,8},{41,9},... | collective-permute-start | bytes 3637256 | tf_op jit(solution)/shard_map/ppermute | solution.py:51
  109.7 10.7 %collective-permute-start.23 = (bf16[32,5120]{1,0:T(8,128)(2,1)S(1)}, bf16[32,5120]{1,0:T(8,128)(2,1)S(1)}, u32[]{:S(2)}, u32[]{:S(2)}) collective-permute-start(bf16[32,5120]{1,0:T(8,128)(2,1)S(1)} %get-tuple-element.116), channel_id=1, source_target_pairs={{96,0},{25,1},{98,2},{27,3},{100,4},{29,5},{102,6},{31,7},{104,8},... | collective-permute-start | bytes 983048 | tf_op jit(solution)/shard_map/ppermute | solution.py:51
  112.3 8.7 %collective-permute-start.24 = (bf16[32,5120]{1,0:T(8,128)(2,1)S(1)}, bf16[32,5120]{1,0:T(8,128)(2,1)S(1)}, u32[]{:S(2)}, u32[]{:S(2)}) collective-permute-start(bf16[32,5120]{1,0:T(8,128)(2,1)S(1)} %get-tuple-element.117), channel_id=1, source_target_pairs={{64,0},{17,1},{66,2},{19,3},{68,4},{21,5},{70,6},{23,7},{72,8},{25... | collective-permute-start | bytes 983048 | tf_op jit(solution)/shard_map/ppermute | solution.py:51
  112.3 11.8 %collective-permute-start.25 = (bf16[32,5120]{1,0:T(8,128)(2,1)S(1)}, bf16[32,5120]{1,0:T(8,128)(2,1)S(1)}, u32[]{:S(2)}, u32[]{:S(2)}) collective-permute-start(bf16[32,5120]{1,0:T(8,128)(2,1)S(1)} %get-tuple-element.118), channel_id=1, source_target_pairs={{32,0},{9,1},{34,2},{11,3},{36,4},{13,5},{38,6},{15,7},{40,8},{17,... | collective-permute-start | bytes 983048 | tf_op jit(solution)/shard_map/ppermute | solution.py:51
  125.0 8.7 %collective-permute-start.26 = (f32[8,5632]{1,0:T(8,128)S(1)}, f32[8,5632]{1,0:T(8,128)S(1)}, u32[]{:S(2)}, u32[]{:S(2)}) collective-permute-start(f32[8,5632]{1,0:T(8,128)S(1)} %get-tuple-element.120), channel_id=1, source_target_pairs={{24,0},{7,1},{26,2},{1,3},{28,4},{3,5},{30,6},{5,7},{0,8},{15,9},{... | collective-permute-start | bytes 540680 | tf_op jit(solution)/shard_map/ppermute | solution.py:51
  125.1 8.6 %collective-permute-start.27 = (f32[8,5632]{1,0:T(8,128)S(1)}, f32[8,5632]{1,0:T(8,128)S(1)}, u32[]{:S(2)}, u32[]{:S(2)}) collective-permute-start(f32[8,5632]{1,0:T(8,128)S(1)} %get-tuple-element.121), channel_id=1, source_target_pairs={{16,0},{5,1},{18,2},{7,3},{20,4},{1,5},{22,6},{3,7},{24,8},{13,9},... | collective-permute-start | bytes 540680 | tf_op jit(solution)/shard_map/ppermute | solution.py:51
  127.4 7.2 %collective-permute-start.28 = (f32[8,5632]{1,0:T(8,128)S(1)}, f32[8,5632]{1,0:T(8,128)S(1)}, u32[]{:S(2)}, u32[]{:S(2)}) collective-permute-start(f32[8,5632]{1,0:T(8,128)S(1)} %get-tuple-element.122), channel_id=1, source_target_pairs={{8,0},{3,1},{10,2},{5,3},{12,4},{7,5},{14,6},{1,7},{16,8},{11,9},{... | collective-permute-start | bytes 540680 | tf_op jit(solution)/shard_map/ppermute | solution.py:51
  134.7 6.9 %collective-permute-start.30 = (f32[8,1024]{1,0:T(8,128)S(1)}, f32[8,1024]{1,0:T(8,128)S(1)}, u32[]{:S(2)}, u32[]{:S(2)}) collective-permute-start(f32[8,1024]{1,0:T(8,128)S(1)} %get-tuple-element.124.refs_0_), channel_id=1, source_target_pairs={{2,0},{33,1},{4,2},{35,3},{6,4},{37,5},{0,6},{39,7},{10,8},{41,9},... | collective-permute-start | bytes 98312 | tf_op jit(solution)/shard_map/ppermute | solution.py:51
  136.7 5.4 %collective-permute-start.31 = (f32[8,1024]{1,0:T(8,128)S(1)}, f32[8,1024]{1,0:T(8,128)S(1)}, u32[]{:S(2)}, u32[]{:S(2)}) collective-permute-start(f32[8,1024]{1,0:T(8,128)S(1)} %get-tuple-element.124.refs_0_), channel_id=1, source_target_pairs={{4,0},{65,1},{6,2},{67,3},{0,4},{69,5},{2,6},{71,7},{12,8},{73,9},... | collective-permute-start | bytes 98312 | tf_op jit(solution)/shard_map/ppermute | solution.py:51
  139.1 4.1 %collective-permute-start.32 = (f32[8,1024]{1,0:T(8,128)S(1)}, f32[8,1024]{1,0:T(8,128)S(1)}, u32[]{:S(2)}, u32[]{:S(2)}) collective-permute-start(f32[8,1024]{1,0:T(8,128)S(1)} %get-tuple-element.124.refs_0_), channel_id=1, source_target_pairs={{6,0},{97,1},{0,2},{99,3},{2,4},{101,5},{4,6},{103,7},{14,8},{105,... | collective-permute-start | bytes 98312 | tf_op jit(solution)/shard_map/ppermute | solution.py:51
  143.2 12.2 %collective-permute-start.33 = (f32[4,8,1024]{2,1,0:T(8,128)S(1)}, f32[4,8,1024]{2,1,0:T(8,128)S(1)}, u32[]{:S(2)}, u32[]{:S(2)}) collective-permute-start(f32[4,8,1024]{2,1,0:T(8,128)S(1)} %collect.3.own), channel_id=1, source_target_pairs={{0,1},{1,0},{2,3},{3,2},{4,5},{5,4},{6,7},{7,6},{8,9},{9,8},{10,11... | collective-permute-start | bytes 393224 | tf_op jit(solution)/shard_map/ppermute | solution.py:56
  143.3 11.5 %collective-permute-start.29 = (f32[8,128]{1,0:T(8,128)S(1)}, f32[8,128]{1,0:T(8,128)S(1)}, u32[]{:S(2)}, u32[]{:S(2)}) collective-permute-start(f32[8,128]{1,0:T(8,128)S(1)} %get-tuple-element.123), channel_id=1, source_target_pairs={{0,0},{1,16},{2,32},{3,17},{4,64},{5,18},{6,96},{7,19},{8,1},{9,20... | collective-permute-start | bytes 12296 | tf_op jit(solution)/shard_map/ppermute | solution.py:509
  (8 other events, 85.5 us)
